TPU v7x, 512 devices: a whole 4x4x16 slice. The times are simulated.
512 devices in a mesh: col: 8 (over z_hi, core), req: 64 (over z_lo, y, x).
Axes of the slice: x: 4, y: 4, z: 16 (z_hi: 4, z_lo: 4; z = z_hi * 4 + z_lo), core: 2. Of those that a mesh axis runs over, the one named last changes fastest.
Arguments:
- event_ids: int32 [131072], P('req'), may hold values from 0 to 32767
- cand_ids: int32 [16384], P('req'), may hold values from 0 to 32767
- cand_request: int32 [16384], P('req'), may hold values from 0 to 63, as said below
- table: bfloat16 [32768, 1024], P(None, 'col'), may hold values from -6 to 6
- w_kv: bfloat16 [1024, 2048], P(None, 'col'), may hold values from -0.1875 to 0.1875
- w_qu: bfloat16 [1024, 2048], P(None, 'col'), may hold values from -0.1875 to 0.1875
- w_out: bfloat16 [1024, 1024], P('col'), may hold values from -0.1875 to 0.1875
Outputs:
- scored: bfloat16 [16384, 1024], P('req', 'col')
Inputs may be any that keep to these rules, and one draw needn't show every extreme that they name: `cand_request`: a candidate held on index i of req belongs to one of the 16 requests whose past events lie on indices 16 * (i // 16) to 16 * (i // 16) + 15 of req.
All inputs are finite; a program needn't handle non-finite values.
Results may differ from a plain program's by a relative error of at most 0.0048.
Values may be sent and summed in bfloat16 or wider, within the bound.
A program may use at most 128 MiB of HBM per device.

v0:
```python
import math

import jax
import jax.numpy as jnp
from jax import lax
from jax.sharding import PartitionSpec as P

D = 1024
DH = 128
GROUP = 16
HIST = 2048
REQ_GROUP = 16


def partner(value, axis, bit):
    return lax.ppermute(value, axis, [(i, i ^ 1 << bit) for i in range(lax.axis_size(axis))])


def attend_rows(running, queries, requests, kv_rows):
    row_count = kv_rows.shape[0]
    width = math.gcd(row_count, HIST)
    block_count = row_count // width
    blocks = kv_rows.reshape(block_count, width, kv_rows.shape[1], 2, DH)
    score_scale = 1.0 / math.sqrt(DH)

    def one_block(total, block_pair):
        block, block_index = block_pair
        scores = (
            jnp.einsum("chd,khd->hck", queries, block[:, :, 0], preferred_element_type=jnp.float32)
            * score_scale
        )
        owner = (block_index * width + jnp.arange(width, dtype=jnp.int32)) // HIST
        allowed = requests[:, None] == owner[None, :]
        weights = jnp.where(allowed[None], jax.nn.silu(scores) / HIST, 0.0).astype(jnp.bfloat16)
        added = jnp.einsum(
            "hck,khd->chd", weights, block[:, :, 1], preferred_element_type=jnp.float32
        )
        return (total + added, None)

    total, _ = lax.scan(one_block, running, (blocks, jnp.arange(block_count, dtype=jnp.int32)))
    return total


def join_ordered(mine, partner_block, upper_bit):
    first = jnp.concatenate([mine, partner_block], 0)
    second = jnp.concatenate([partner_block, mine], 0)
    return jnp.where(upper_bit == 0, first, second)


def on_device(event_ids, cand_ids, cand_request, table, w_kv, w_qu, w_out):
    group_width = w_kv.shape[1]
    heads_here = group_width // (2 * DH)
    cand_count = cand_ids.shape[0]
    event_count = event_ids.shape[0]
    hist_slice = jnp.take(table, event_ids, axis=0)
    cand_slice = jnp.take(table, cand_ids, axis=0)
    kv_total = jnp.dot(
        lax.all_gather(hist_slice, "col", axis=1, tiled=True),
        w_kv,
        preferred_element_type=jnp.float32,
    )
    qu_total = jnp.dot(
        lax.all_gather(cand_slice, "col", axis=1, tiled=True),
        w_qu,
        preferred_element_type=jnp.float32,
    )
    history = kv_total.astype(jnp.bfloat16).reshape(event_count, heads_here, 2, DH)
    projected = qu_total.reshape(cand_count, heads_here, 2, DH)
    queries = projected[:, :, 0].astype(jnp.bfloat16)
    gating = jax.nn.silu(projected[:, :, 1])
    requests = cand_request % REQ_GROUP
    position = lax.axis_index("req") % GROUP
    bit_count = GROUP.bit_length() - 1
    start_value = jnp.zeros((cand_count, heads_here, DH), jnp.float32)
    gathered = history
    for bit_index in range(bit_count):
        partner_block = partner(gathered, "req", bit_index)
        upper_bit = position // (1 << bit_index) % 2
        gathered = join_ordered(gathered, partner_block, upper_bit)
    attended = attend_rows(start_value, queries, requests, gathered)
    features = attended.reshape(cand_count, heads_here * DH)
    moments = lax.psum((jnp.sum(features, 1), jnp.sum(features * features, 1)), "col")
    average = moments[0] / D
    variance = moments[1] / D - average * average
    normed = (features - average[:, None]) * lax.rsqrt(variance[:, None] + 1e-05)
    gated = (normed * gating.reshape(cand_count, heads_here * DH)).astype(jnp.bfloat16)
    out_cols = lax.psum_scatter(
        lax.dot_general(w_out, gated, (((0,), (1,)), ((), ())), preferred_element_type=jnp.float32),
        "col",
        scatter_dimension=0,
        tiled=True,
    )
    return (cand_slice.astype(jnp.float32) + out_cols.T).astype(jnp.bfloat16)


def solution(mesh):
    in_specs = (
        P("req"),
        P("req"),
        P("req"),
        P(None, "col"),
        P(None, "col"),
        P(None, "col"),
        P("col", None),
    )
    out_specs = P("req", "col")
    return jax.shard_map(
        on_device, mesh=mesh, in_specs=in_specs, out_specs=out_specs, check_vma=False
    )
```

profile of v0, /device:TPU:1, one launch (start us, length us, event | category | flops | bytes accessed | tf_op | source)
XLA Modules:
  0.0 685.9 jit_solution(10618973729634520110)
XLA Ops:
  6.5 0.8 fusion.30
  7.3 0.7 compare_and_fusion
  8.0 10.1 %gather_fusion.1 = bf16[2048,128]{1,0:T(8,128)(2,1)S(1)} fusion(bf16[32768,128]{1,0:T(8,128)(2,1)} %param.12, s32[2048]{0:T(1024)S(1)} %fusion.30), kind=kCustom, calls=%fused_computation.1 | custom fusion | bytes 1056768 | tf_op jit(solution)/shard_map/jit(_take)/gather | solution.py:55
  18.1 1.2 broadcast_select_fusion
  19.3 107.3 %all-gather.2.cloned.1.call-done = bf16[2048,1024]{1,0:T(8,128)(2,1)} async-done(((bf16[2048,128]{1,0:T(8,128)(2,1)}), bf16[2048,1024]{1,0:T(8,128)(2,1)}) %all-gather.2.cloned.1.call-update) | async-done | bytes 4194320 | tf_op jit(solution)/shard_map/all_gather | solution.py:58
  126.6 3.5 convolution_convert_fusion
  130.1 1.0 copy-done.3
  131.1 0.7 copy.11
  131.8 3.2 collective-permute-start
  135.0 23.1 %collective-permute-done = bf16[2048,1,2,128]{3,0,2,1:T(8,128)(2,1)S(1)} collective-permute-done((bf16[2048,1,2,128]{3,0,2,1:T(8,128)(2,1)S(1)}, bf16[2048,1,2,128]{3,0,2,1:T(8,128)(2,1)S(1)}, u32[]{:S(2)}, u32[]{:S(2)}) %collective-permute-start) | collective-permute-done | bytes 1048608 | tf_op jit(solution)/shard_map/ppermute | solution.py:16
  158.2 1.9 maximum_select_fusion.5
  160.0 4.8 collective-permute-start.1
  164.8 2.3 copy.12
  167.1 2.8 maximum_select_fusion.4
  169.9 39.9 %collective-permute-done.1 = bf16[4096,1,2,128]{3,0,2,1:T(8,128)(2,1)} collective-permute-done((bf16[4096,1,2,128]{3,0,2,1:T(8,128)(2,1)}, bf16[4096,1,2,128]{3,0,2,1:T(8,128)(2,1)}, u32[]{:S(2)}, u32[]{:S(2)}) %collective-permute-start.1) | collective-permute-done | bytes 2097184 | tf_op jit(solution)/shard_map/ppermute | solution.py:16
  209.8 4.8 maximum_select_fusion.3
  214.6 3.4 collective-permute-start.2
  218.0 3.4 fusion.19
  221.5 85.4 %collective-permute-done.2 = bf16[8192,1,2,128]{3,0,2,1:T(8,128)(2,1)} collective-permute-done((bf16[8192,1,2,128]{3,0,2,1:T(8,128)(2,1)}, bf16[8192,1,2,128]{3,0,2,1:T(8,128)(2,1)}, u32[]{:S(2)}, u32[]{:S(2)}) %collective-permute-start.2) | collective-permute-done | bytes 4194336 | tf_op jit(solution)/shard_map/ppermute | solution.py:16
  306.8 32.2 %maximum_select_fusion.1 = bf16[16384,1,2,128]{3,0,2,1:T(8,128)(2,1)} fusion(bf16[8192,1,2,128]{3,0,2,1:T(8,128)(2,1)} %collective-permute-done.2, bf16[8192,1,2,128]{3,0,2,1:T(8,128)(2,1)S(1)} %fusion.19, pred[]{:T(512)S(6)} %eq.44), kind=kLoop, calls=%fused_computation.32 | loop fusion | flops 37748736 | bytes 16777216 | tf_op jit(solution)/shard_map/jit(_where)/select_n | solution.py:47
  339.0 4.8 collective-permute-start.3
  343.9 5.2 gather_fusion
  349.2 24.2 %all_gather.7 = bf16[256,1024]{1,0:T(8,128)(2,1)S(1)} all-gather(bf16[256,128]{1,0:T(8,128)(2,1)S(1)} %broadcast_select_fusion.1), channel_id=1, replica_groups=mesh['col'=8,'req'=64] {'col'}, dimensions={1}, use_global_device_ids=true | all-gather | bytes 589824 | tf_op jit(solution)/shard_map/all_gather | solution.py:63
  373.9 147.8 %collective-permute-done.3 = bf16[16384,1,2,128]{3,0,2,1:T(8,128)(2,1)} collective-permute-done((bf16[16384,1,2,128]{3,0,2,1:T(8,128)(2,1)}, bf16[16384,1,2,128]{3,0,2,1:T(8,128)(2,1)}, u32[]{:S(2)}, u32[]{:S(2)}) %collective-permute-start.3) | collective-permute-done | bytes 8388640 | tf_op jit(solution)/shard_map/ppermute | solution.py:16
  521.8 23.8 %maximum_select_fusion = bf16[32768,1,2,128]{3,0,2,1:T(8,128)(2,1)} fusion(bf16[16384,1,2,128]{3,0,2,1:T(8,128)(2,1)} %collective-permute-done.3, bf16[16384,1,2,128]{3,0,2,1:T(8,128)(2,1)} %maximum_select_fusion.1, pred[]{:T(512)S(6)} %eq.43), kind=kLoop, calls=%fused_computation.31 | loop fusion | flops 75497472 | bytes 33554432 | tf_op jit(solution)/shard_map/jit(_where)/select_n | solution.py:47
  545.6 58.7 %while.13 = (s32[]{:T(128)}, f32[256,1,128]{0,2,1:T(8,128)S(1)}, bf16[16,2048,1,2,128]{4,1,0,3,2:T(8,128)(2,1)}, s32[256]{0:T(256)S(1)}, s32[16]{0:T(128)S(1)}, ...) while((s32[]{:T(128)}, f32[256,1,128]{0,2,1:T(8,128)S(1)}, ...), condition=%wide.region_1.2_spmd.clone, body=%wide.region_0.1_spmd.clone.sunk | while | flops 273252352 | bytes 3490951 | solution.py:40
  545.6 0.6 dynamic_slice.20
  546.8 1.3 dynamic-slice_bitcast_fusion.2
  548.1 1.1 fusion.42
  550.5 1.3 dynamic-slice_bitcast_fusion.2
  551.8 1.1 fusion.42
  554.2 1.3 dynamic-slice_bitcast_fusion.2
  555.5 1.1 fusion.42
  556.6 0.6 dynamic_slice.20
  557.8 1.3 dynamic-slice_bitcast_fusion.2
  559.1 1.1 fusion.42
  561.5 1.3 dynamic-slice_bitcast_fusion.2
  562.8 1.1 fusion.42
  565.2 1.3 dynamic-slice_bitcast_fusion.2
  566.5 1.1 fusion.42
  568.8 1.3 dynamic-slice_bitcast_fusion.2
  570.1 1.1 fusion.42
  572.5 1.3 dynamic-slice_bitcast_fusion.2
  573.8 1.1 fusion.42
  576.2 1.3 dynamic-slice_bitcast_fusion.2
  577.5 1.1 fusion.42
  579.9 1.3 dynamic-slice_bitcast_fusion.2
  581.2 1.1 fusion.42
  583.5 1.3 dynamic-slice_bitcast_fusion.2
  584.8 1.1 fusion.42
  587.2 1.3 dynamic-slice_bitcast_fusion.2
  588.5 1.1 fusion.42
  590.9 1.3 dynamic-slice_bitcast_fusion.2
  592.2 1.1 fusion.42
  594.5 1.3 dynamic-slice_bitcast_fusion.2
  595.9 1.1 fusion.42
  598.2 1.3 dynamic-slice_bitcast_fusion.2
  599.5 1.1 fusion.42
  601.9 1.3 dynamic-slice_bitcast_fusion.2
  603.2 1.1 fusion.42
  604.4 21.1 %all-reduce = (f32[256]{0:T(256)S(1)}, f32[256]{0:T(256)S(1)}) all-reduce(f32[256]{0:T(256)S(1)} %fusion.24, f32[256]{0:T(256)S(1)} %reduce_sum.18), channel_id=1, replica_groups=mesh['col'=8,'req'=64] {'col'}, use_global_device_ids=true, to_apply=%region_5.6 | all-reduce | flops 512 | bytes 4096 | tf_op jit(solution)/shard_map/psum | solution.py:82
  625.5 1.3 convolution_bitcast_fusion
  626.9 50.6 %reduce-scatter.2.cloned.1.call-done = f32[128,256]{0,1:T(8,128)} async-done(((f32[1024,256]{0,1:T(8,128)}), f32[128,256]{0,1:T(8,128)}) %reduce-scatter.2.cloned.1.call-update) | async-done | bytes 131088 | tf_op jit(solution)/shard_map/reduce_scatter | solution.py:87
  677.5 1.6 fusion.20
  (62 shorter events, 9.3 us)
Async XLA Ops:
  6.5 120.1 %copy-start = (bf16[1024,256]{1,0:T(8,128)(2,1)S(1)}, bf16[1024,256]{1,0:T(8,128)(2,1)}, u32[]{:S(2)}) copy-start(bf16[1024,256]{1,0:T(8,128)(2,1)} %param.13) | copy-start | bytes 1572868
  6.5 120.1 %all-gather.2.cloned.1.call-start = ((), (), s32[]{:S(2)}) async-start(), calls=%async_computation.1 | async-start | bytes 4718592 | tf_op jit(solution)/shard_map/all_gather | solution.py:58
  19.2 658.2 %reduce-scatter.2.cloned.1.call-start = ((), (), s32[]{:S(2)}) async-start(), calls=%async_computation.2 | async-start | bytes 1179648 | tf_op jit(solution)/shard_map/reduce_scatter | solution.py:87
  130.1 1.0 copy-start.3
  131.8 26.4 %collective-permute-start = (bf16[2048,1,2,128]{3,0,2,1:T(8,128)(2,1)S(1)}, bf16[2048,1,2,128]{3,0,2,1:T(8,128)(2,1)S(1)}, u32[]{:S(2)}, u32[]{:S(2)}) collective-permute-start(bf16[2048,1,2,128]{3,0,2,1:T(8,128)(2,1)S(1)} %copy.11), channel_id=1, source_target_pairs={{0,1},{1,0},{2,3},{3,2},{4,5},{5,4},{6,7},{7,6},{8,9},{9,8},{10,11... | collective-permute-start | bytes 3145736 | tf_op jit(solution)/shard_map/ppermute | solution.py:16
  158.2 9.0 %copy-start.2 = (bf16[2048,1,2,128]{3,0,2,1:T(8,128)(2,1)}, bf16[2048,1,2,128]{3,0,2,1:T(8,128)(2,1)S(1)}, u32[]{:S(2)}) copy-start(bf16[2048,1,2,128]{3,0,2,1:T(8,128)(2,1)S(1)} %collective-permute-done) | copy-start | bytes 3145732
  160.0 49.8 %collective-permute-start.1 = (bf16[4096,1,2,128]{3,0,2,1:T(8,128)(2,1)}, bf16[4096,1,2,128]{3,0,2,1:T(8,128)(2,1)}, u32[]{:S(2)}, u32[]{:S(2)}) collective-permute-start(bf16[4096,1,2,128]{3,0,2,1:T(8,128)(2,1)} %maximum_select_fusion.5), channel_id=1, source_target_pairs={{0,2},{1,3},{2,0},{3,1},{4,6},{5,7},{6,4},{7,5},{8,10},{9,11},{10,... | collective-permute-start | bytes 6291464 | tf_op jit(solution)/shard_map/ppermute | solution.py:16
  214.6 92.3 %collective-permute-start.2 = (bf16[8192,1,2,128]{3,0,2,1:T(8,128)(2,1)}, bf16[8192,1,2,128]{3,0,2,1:T(8,128)(2,1)}, u32[]{:S(2)}, u32[]{:S(2)}) collective-permute-start(bf16[8192,1,2,128]{3,0,2,1:T(8,128)(2,1)} %maximum_select_fusion.3), channel_id=1, source_target_pairs={{0,4},{1,5},{2,6},{3,7},{4,0},{5,1},{6,2},{7,3},{8,12},{9,13},{10,... | collective-permute-start | bytes 12582920 | tf_op jit(solution)/shard_map/ppermute | solution.py:16
  221.4 122.4 %copy-start.6 = (s32[256]{0:T(256)S(1)}, s32[256]{0:T(256)}, u32[]{:S(2)}) copy-start(s32[256]{0:T(256)} %param.10) | copy-start | bytes 3076
  221.4 152.0 %copy-start.4 = (bf16[1024,256]{1,0:T(8,128)(2,1)S(1)}, bf16[1024,256]{1,0:T(8,128)(2,1)}, u32[]{:S(2)}) copy-start(bf16[1024,256]{1,0:T(8,128)(2,1)} %param.14) | copy-start | bytes 1572868
  221.4 152.5 %copy-start.7 = (s32[256]{0:T(256)S(1)}, s32[256]{0:T(256)}, u32[]{:S(2)}) copy-start(s32[256]{0:T(256)} %param.11) | copy-start | bytes 3076
  339.0 182.7 %collective-permute-start.3 = (bf16[16384,1,2,128]{3,0,2,1:T(8,128)(2,1)}, bf16[16384,1,2,128]{3,0,2,1:T(8,128)(2,1)}, u32[]{:S(2)}, u32[]{:S(2)}) collective-permute-start(bf16[16384,1,2,128]{3,0,2,1:T(8,128)(2,1)} %maximum_select_fusion.1), channel_id=1, source_target_pairs={{0,8},{1,9},{2,10},{3,11},{4,12},{5,13},{6,14},{7,15},{8,0},{9,1},... | collective-permute-start | bytes 25165832 | tf_op jit(solution)/shard_map/ppermute | solution.py:16
  545.5 80.0 %copy-start.5 = (bf16[128,1024]{1,0:T(8,128)(2,1)S(1)}, bf16[128,1024]{1,0:T(8,128)(2,1)}, u32[]{:S(2)}) copy-start(bf16[128,1024]{1,0:T(8,128)(2,1)} %param.15) | copy-start | bytes 786436
  604.3 74.8 %copy-start.1 = (bf16[1024,256]{1,0:T(8,128)(2,1)S(1)}, bf16[1024,256]{1,0:T(8,128)(2,1)}, u32[]{:S(2)}) copy-start(bf16[1024,256]{1,0:T(8,128)(2,1)} %param.13) | copy-start | bytes 1572868
Sparse Core Ops, SparseCore 0:
  19.4 107.2 all-gather.1
  627.0 50.4 reduce-scatter.1
where the time goes:
time: 689 us; the launch traced here: 686 us
  waiting for transfers between devices  454 us (66%)
  other arithmetic  73.4 us (11%)
  local copies, waits for them, and re-layouts  49.7 us (7%)
  blocking collectives  45.4 us (7%)
  matrix products  22.6 us (3%)
  starting transfers between devices  16.2 us (2%)
  between operations  13.8 us (2%)
  loops' own time  10.6 us (2%)
    ppermute x4, waiting for transfers between devices, partner(): lax.ppermute(value, axis, [(i, i ^ 1 << bit) for i in range(lax.axis_size...  296 us
    all_gather x1, waiting for transfers between devices, on_device(): lax.all_gather(hist_slice, 'col', axis=1, tiled=True)  107 us
    select_n x5, other arithmetic, join_ordered(): return jnp.where(upper_bit == 0, first, second)  65.4 us
    reduce_scatter x1, waiting for transfers between devices, on_device(): lax.psum_scatter(lax.dot_general(w_out, gated, (((0,), (1,)), ((), ())),...  50.6 us
    all_gather x1, blocking collectives, on_device(): lax.all_gather(cand_slice, 'col', axis=1, tiled=True)  24.2 us
    psum x1, blocking collectives, on_device(): lax.psum((jnp.sum(features, 1), jnp.sum(features * features, 1)), 'col')  21.1 us
    squeeze x16, local copies, waits for them, and re-layouts, attend_rows(): lax.scan(one_block, running, (blocks, jnp.arange(block_count, dtype=jnp.i...  20.9 us
    dot_general x16, matrix products, one_block(): jnp.einsum('hck,khd->chd', weights, block[:, :, 1], preferred_element_typ...  17.5 us
  transfers between devices with their start and end apart: 6, of which 6 were waited for; matrix products, arithmetic and copies ran while one was open for 2% of the time, Pallas kernels for 0%

commit v1 on v0

v1 whole, which is shorter than its diff:
```python
import functools
import math

import jax
import jax.numpy as jnp
from jax import lax
from jax.experimental import pallas as pl
from jax.experimental.pallas import tpu as pltpu
from jax.sharding import PartitionSpec as P

D = 1024
DH = 128
GROUP = 16
HIST = 2048
REQ_GROUP = 16
CHUNK = 2048
CAND = 256
PIECES = 8
ROWS = CHUNK // PIECES
LAG = 1
PAIR = 2 * CAND
TILE = 512
MESH = pl.DeviceIdType.MESH
NT = (((1,), (1,)), ((), ()))


def attend_kernel(
    table, w_kv, q_in, msg_in, att_out,
    rows, keys, values, queries, msgs, counts, onehot, parts_out, parts_in, own_part,
    own_sem, ring_send, ring_recv, pair_send, pair_recv,
    q_send, q_recv, m_send, m_recv, p_send, p_recv, local_sem,
):
    col, req = lax.axis_index("col"), lax.axis_index("req")
    z_hi, core = col // 2, col % 2
    z_lo, me = req // 16, req % 16
    z = z_hi * 4 + z_lo

    def at_z(other):
        other = lax.rem(other + 16, 16)
        return (other // 4 * 2 + core, other % 4 * 16 + me)

    above, below = at_z(z + 1), at_z(z - 1)
    sibling = (z_hi * 2 + 1 - core, req)

    def peer(index):
        return (col, z_lo * 16 + index)

    barrier = pltpu.get_barrier_semaphore()
    for other in (above, below, sibling):
        pl.semaphore_signal(barrier, inc=1, device_id=other, device_id_type=MESH)

    def greet(j, carry):
        pl.semaphore_signal(
            barrier, inc=1, device_id=peer(lax.rem(me + j, 16)), device_id_type=MESH
        )
        return carry

    lax.fori_loop(1, 16, greet, 0)

    def place(block, half, p):
        return rows.at[
            pl.ds(pl.multiple_of(p * ROWS, ROWS), ROWS),
            pl.ds(pl.multiple_of((block * 2 + half) * 128, 128), 128),
        ]

    def own_copy(p):
        start = pl.multiple_of(me * CHUNK + p * ROWS, ROWS)
        return pltpu.make_async_copy(
            table.at[pl.ds(start, ROWS), :], place(z_hi, core, p), own_sem.at[p]
        )

    for p in range(PIECES):
        own_copy(p).start()
    q_own = pltpu.make_async_copy(
        q_in, queries.at[pl.ds(pl.multiple_of(me * CAND, CAND), CAND), :], local_sem.at[0]
    )
    m_own = pltpu.make_async_copy(msg_in.at[me], msgs.at[me], local_sem.at[1])
    q_own.start()
    m_own.start()
    pl.semaphore_wait(barrier, 18)

    below_block, above_block = lax.rem(z_hi + 3, 4), lax.rem(z_hi + 1, 4)
    far_block = lax.rem(z_hi + 2, 4)

    def ring(block, p, target, sent, kind):
        return pltpu.make_async_remote_copy(
            src_ref=place(block, core, p),
            dst_ref=place(block, core, p),
            send_sem=ring_send.at[sent, p],
            recv_sem=ring_recv.at[kind, p],
            device_id=target,
            device_id_type=MESH,
        )

    def across(block, p, slot):
        return pltpu.make_async_remote_copy(
            src_ref=place(block, core, p),
            dst_ref=place(block, core, p),
            send_sem=pair_send.at[slot, p],
            recv_sem=pair_recv.at[slot, p],
            device_id=sibling,
            device_id_type=MESH,
        )

    def send_own(p, carry):
        own_copy(p).wait()

        @pl.when(z_lo == 3)
        def _():
            ring(z_hi, p, above, 0, 0).start()

        @pl.when(z_lo == 0)
        def _():
            ring(z_hi, p, below, 1, 1).start()

        across(z_hi, p, 0).start()
        return carry

    lax.fori_loop(0, PIECES, send_own, 0)

    def q_copy(j, slot):
        return pltpu.make_async_remote_copy(
            src_ref=q_in,
            dst_ref=queries.at[pl.ds(pl.multiple_of(slot * CAND, CAND), CAND), :],
            send_sem=q_send.at[j],
            recv_sem=q_recv.at[slot],
            device_id=peer(lax.rem(me + j, 16)),
            device_id_type=MESH,
        )

    def m_copy(j, slot):
        to = lax.rem(me + j, 16)
        return pltpu.make_async_remote_copy(
            src_ref=msg_in.at[to],
            dst_ref=msgs.at[slot],
            send_sem=m_send.at[j],
            recv_sem=m_recv.at[slot],
            device_id=peer(to),
            device_id_type=MESH,
        )

    def spread(j, carry):
        m_copy(j, me).start()
        q_copy(j, me).start()
        return carry

    lax.fori_loop(1, 16, spread, 0)

    def ring_step(t, carry):
        @pl.when(t < PIECES)
        def _():
            p = t
            even = lax.rem(p, 2) == 0
            ring(below_block, p, below, 0, 0).wait_recv()

            @pl.when((z_lo < 3) | even)
            def _():
                @pl.when(z_lo < 3)
                def _():
                    ring(below_block, p, above, 0, 0).start()

                @pl.when(z_lo == 3)
                def _():
                    ring(below_block, p, above, 2, 2).start()

            across(below_block, p, 1).start()
            ring(above_block, p, above, 1, 1).wait_recv()

            @pl.when(z_lo > 0)
            def _():
                ring(above_block, p, below, 1, 1).start()

            @pl.when((z_lo == 0) & jnp.logical_not(even))
            def _():
                ring(above_block, p, below, 2, 2).start()

            across(above_block, p, 2).start()

        @pl.when((t >= LAG) & (t < PIECES + LAG))
        def _():
            p = jnp.maximum(t - LAG, 0)
            even = lax.rem(p, 2) == 0
            ring(far_block, p, above, 2, 2).wait_recv()

            @pl.when(even & (z_lo < 3))
            def _():
                ring(far_block, p, above, 2, 2).start()

            @pl.when(jnp.logical_not(even) & (z_lo > 0))
            def _():
                ring(far_block, p, below, 2, 2).start()

            across(far_block, p, 3).start()

        @pl.when(t >= 2 * LAG)
        def _():
            p = jnp.maximum(t - 2 * LAG, 0)
            across(z_hi, p, 0).wait_recv()
            across(below_block, p, 1).wait_recv()
            across(above_block, p, 2).wait_recv()
            across(far_block, p, 3).wait_recv()
            here = pl.ds(pl.multiple_of(p * ROWS, ROWS), ROWS)
            both = jnp.dot(rows[here, :], w_kv[...], preferred_element_type=jnp.float32)
            both = both.astype(jnp.bfloat16)
            keys[here, :] = both[:, :DH]
            values[here, :] = both[:, DH:]

        return carry

    lax.fori_loop(0, PIECES + 2 * LAG, ring_step, 0)

    q_own.wait()
    m_own.wait()

    def arrived(j, carry):
        src = lax.rem(me + j, 16)
        m_copy(j, src).wait_recv()
        q_copy(j, src).wait_recv()
        return carry

    lax.fori_loop(1, 16, arrived, 0)
    for s in range(8):
        count = msgs[:, s, :]
        high = jnp.floor(count * (1.0 / 256.0))
        low = count - high * 256.0
        counts[:, s * 256 : (s + 1) * 256] = jnp.concatenate(
            [low, high, jnp.zeros((96, 256), jnp.float32)], 0
        ).astype(jnp.bfloat16)

    def mark(src, carry):
        wanted = msgs[src, 8:9, :]
        lane = lax.broadcasted_iota(jnp.int32, (DH, CAND), 0).astype(jnp.float32)
        hot = jnp.where(lane == wanted, 1.0, 0.0) + jnp.where(lane == wanted + 16.0, 256.0, 0.0)
        onehot[pl.ds(pl.multiple_of(src * CAND, CAND), CAND), :] = hot.T.astype(jnp.bfloat16)
        return carry

    lax.fori_loop(0, 16, mark, 0)

    half_scale = 0.5 / math.sqrt(DH)

    def part_copy(to, slot):
        return pltpu.make_async_remote_copy(
            src_ref=parts_out.at[to],
            dst_ref=parts_in.at[slot],
            send_sem=p_send.at[to],
            recv_sem=p_recv.at[slot],
            device_id=peer(to),
            device_id_type=MESH,
        )

    def attend_pair(i, carry):
        pair = lax.rem(me // 2 + 1 + i, 8)
        here = pl.ds(pl.multiple_of(pair * PAIR, PAIR), PAIR)
        picked, hot = queries[here, :], onehot[here, :]
        total = jnp.zeros((PAIR, DH), jnp.float32)
        for r in range(CHUNK // TILE):
            span = slice(r * TILE, (r + 1) * TILE)
            u = lax.dot_general(picked, keys[span, :], NT, preferred_element_type=jnp.float32)
            times = jnp.dot(hot, counts[:, span], preferred_element_type=jnp.float32)
            u = u * half_scale
            weight = ((u + u * jnp.tanh(u)) * times).astype(jnp.bfloat16)
            total += jnp.dot(weight, values[span, :], preferred_element_type=jnp.float32)
        for k in range(2):
            src = pair * 2 + k
            part = total[k * CAND : (k + 1) * CAND]

            @pl.when(src == me)
            def _():
                own_part[...] = part

            @pl.when(src != me)
            def _():
                parts_out[src] = part.astype(jnp.bfloat16)
                part_copy(src, me).start()

        return carry

    lax.fori_loop(0, 8, attend_pair, 0)

    def collect(j, total):
        src = lax.rem(me + j, 16)
        part_copy(src, src).wait_recv()
        own_part[...] += parts_in[src].astype(jnp.float32)
        return total

    lax.fori_loop(1, 16, collect, 0)
    att_out[...] = own_part[...] * (1.0 / HIST)

    def sent_ring(p, carry):
        even = lax.rem(p, 2) == 0

        @pl.when(z_lo == 3)
        def _():
            ring(z_hi, p, above, 0, 0).wait_send()

        @pl.when(z_lo < 3)
        def _():
            ring(below_block, p, above, 0, 0).wait_send()

        @pl.when(z_lo == 0)
        def _():
            ring(z_hi, p, below, 1, 1).wait_send()

        @pl.when(z_lo > 0)
        def _():
            ring(above_block, p, below, 1, 1).wait_send()

        @pl.when(even)
        def _():
            ring(far_block, p, above, 2, 2).wait_send()

        @pl.when(jnp.logical_not(even))
        def _():
            ring(far_block, p, below, 2, 2).wait_send()

        for slot in range(4):
            across(far_block, p, slot).wait_send()
        return carry

    lax.fori_loop(0, PIECES, sent_ring, 0)

    def sent_plane(j, carry):
        m_copy(j, me).wait_send()
        q_copy(j, me).wait_send()
        part_copy(lax.rem(me + j, 16), me).wait_send()
        return carry

    lax.fori_loop(1, 16, sent_plane, 0)


def attended_parts(table, w_kv, queries, msg):
    vmem = pl.BlockSpec(memory_space=pltpu.VMEM)
    dma = pltpu.SemaphoreType.DMA
    return pl.pallas_call(
        attend_kernel,
        out_shape=jax.ShapeDtypeStruct((CAND, DH), jnp.float32),
        in_specs=[pl.BlockSpec(memory_space=pl.ANY), vmem, vmem, vmem],
        out_specs=vmem,
        scratch_shapes=[
            pltpu.VMEM((CHUNK, D), jnp.bfloat16),
            pltpu.VMEM((CHUNK, DH), jnp.bfloat16),
            pltpu.VMEM((CHUNK, DH), jnp.bfloat16),
            pltpu.VMEM((16 * CAND, DH), jnp.bfloat16),
            pltpu.VMEM((16, 16, CAND), jnp.float32),
            pltpu.VMEM((DH, CHUNK), jnp.bfloat16),
            pltpu.VMEM((16 * CAND, DH), jnp.bfloat16),
            pltpu.VMEM((16, CAND, DH), jnp.bfloat16),
            pltpu.VMEM((16, CAND, DH), jnp.bfloat16),
            pltpu.VMEM((CAND, DH), jnp.float32),
            dma((PIECES,)),
            dma((3, PIECES)),
            dma((3, PIECES)),
            dma((4, PIECES)),
            dma((4, PIECES)),
            dma((16,)),
            dma((16,)),
            dma((16,)),
            dma((16,)),
            dma((16,)),
            dma((16,)),
            dma((2,)),
        ],
        compiler_params=pltpu.CompilerParams(
            collective_id=0, has_side_effects=True, vmem_limit_bytes=48 << 20
        ),
        cost_estimate=pl.CostEstimate(
            flops=7 << 30, bytes_accessed=4 << 20, transcendentals=8 << 20
        ),
        name="attend_chunk",
    )(table, w_kv, queries, msg)


def on_device(event_ids, cand_ids, cand_request, table, w_kv, w_qu, w_out):
    cand_slice = jnp.take(table, cand_ids, axis=0)
    projected = jnp.dot(
        lax.all_gather(cand_slice, "col", axis=1, tiled=True),
        w_qu,
        preferred_element_type=jnp.float32,
    )
    queries = projected[:, :DH].astype(jnp.bfloat16)
    gating = jax.nn.silu(projected[:, DH:])
    high = (event_ids[None, :] // 128 == jnp.arange(256, dtype=jnp.int32)[:, None]).astype(
        jnp.bfloat16
    )
    low = (event_ids[None, :] % 128 == jnp.arange(128, dtype=jnp.int32)[:, None]).astype(
        jnp.bfloat16
    )
    times = lax.dot_general(high, low, NT, preferred_element_type=jnp.float32)
    wanted = (cand_request % REQ_GROUP).astype(jnp.float32)
    msg = jnp.concatenate(
        [times.reshape(16, 8, 256), jnp.broadcast_to(wanted[None, None, :], (16, 8, 256))], 1
    )
    features = attended_parts(table, w_kv, queries, msg)
    moments = lax.psum((jnp.sum(features, 1), jnp.sum(features * features, 1)), "col")
    average = moments[0] / D
    variance = moments[1] / D - average * average
    normed = (features - average[:, None]) * lax.rsqrt(variance[:, None] + 1e-05)
    gated = (normed * gating).astype(jnp.bfloat16)
    out_cols = lax.psum_scatter(
        lax.dot_general(w_out, gated, (((0,), (1,)), ((), ())), preferred_element_type=jnp.float32),
        "col",
        scatter_dimension=0,
        tiled=True,
    )
    return (cand_slice.astype(jnp.float32) + out_cols.T).astype(jnp.bfloat16)


def solution(mesh):
    in_specs = (
        P("req"),
        P("req"),
        P("req"),
        P(None, "col"),
        P(None, "col"),
        P(None, "col"),
        P("col", None),
    )
    out_specs = P("req", "col")
    return jax.shard_map(
        on_device, mesh=mesh, in_specs=in_specs, out_specs=out_specs, check_vma=False
    )
```

time: 689 us -> 356 us (0.52)
  waiting for transfers between devices: 454 us -> 53.3 us
  Pallas kernels: 0 us -> 220 us
  other arithmetic: 73.4 us -> 4.74 us
  local copies, waits for them, and re-layouts: 49.7 us -> 6.3 us
  matrix products: 22.6 us -> 2.2 us
  starting transfers between devices: 16.2 us -> 0.01 us
  loops' own time: 10.6 us -> 0 us
  blocking collectives: 45.4 us -> 52.8 us
    ppermute x4 -> x0, waiting for transfers between devices: 296 us -> none  [partner(): lax.ppermute(value, axis, [(i, i ^ 1 << bit) for i in range(lax.axis_size...]
    pallas_call x0 -> x1, Pallas kernels: none -> 220 us  [attended_parts(): pl.pallas_call(attend_kernel, out_shape=jax.ShapeDtypeStruct((CAND, DH),...]
    all_gather x1 -> x0, waiting for transfers between devices: 107 us -> none  [on_device(): lax.all_gather(hist_slice, 'col', axis=1, tiled=True)]
    select_n x23 -> x1, other arithmetic: 66.7 us -> 0.71 us  [on_device(): event_ids[None, :] % 128 == jnp.arange(128, dtype=jnp.int32)[:, None]]
    squeeze x16 -> x0, local copies, waits for them, and re-layouts: 20.9 us -> none  [attend_rows(): lax.scan(one_block, running, (blocks, jnp.arange(block_count, dtype=jnp.i...]
    dot_general x17 -> x1, matrix products: 21 us -> 0.55 us  [on_device(): times = lax.dot_general(high, low, NT, preferred_element_type=jnp.float32)]
    ppermute x4 -> x0, starting transfers between devices: 16.2 us -> none  [partner(): lax.ppermute(value, axis, [(i, i ^ 1 << bit) for i in range(lax.axis_size...]
    all_gather x1, blocking collectives: 24.2 us -> 35.2 us  [on_device(): lax.all_gather(cand_slice, 'col', axis=1, tiled=True)]
  transfers between devices with their start and end apart: 6 -> 1, of which waited for: 6 -> 1; matrix products, arithmetic and copies ran while one was open for 2% -> 0% of each run, Pallas kernels for 0% -> 0%
where the time goes in v1:
time: 356 us; the launch traced here: 353 us
  Pallas kernels  220 us (62%)
  waiting for transfers between devices  53.3 us (15%)
  blocking collectives  52.8 us (15%)
  between operations  13.5 us (4%)
  local copies, waits for them, and re-layouts  6.3 us (2%)
  other arithmetic  4.74 us (1%)
    pallas_call x1, Pallas kernels, attended_parts(): pl.pallas_call(attend_kernel, out_shape=jax.ShapeDtypeStruct((CAND, DH),...  220 us
    reduce_scatter x1, waiting for transfers between devices, on_device(): lax.psum_scatter(lax.dot_general(w_out, gated, (((0,), (1,)), ((), ())),...  53.3 us
    all_gather x1, blocking collectives, on_device(): lax.all_gather(cand_slice, 'col', axis=1, tiled=True)  35.2 us
    psum x1, blocking collectives, on_device(): lax.psum((jnp.sum(features, 1), jnp.sum(features * features, 1)), 'col')  17.6 us
  transfers between devices with their start and end apart: 1, of which 1 were waited for; matrix products, arithmetic and copies ran while one was open for 0% of the time, Pallas kernels for 0%

profile of v1, /device:TPU:1, one launch (start us, length us, event | category | flops | bytes accessed | tf_op | source)
XLA Modules:
  0.0 353.1 jit_solution(17834414865700517295)
XLA Ops:
  6.5 0.0 copy-start
  6.5 0.0 reduce-scatter.2.cloned.1.call-start
  6.5 0.7 compare_and_fusion
  7.3 0.7 compare_select_fusion
  8.0 0.7 fusion.9
  8.7 0.7 add_select_fusion
  9.4 0.5 fusion
  10.0 5.2 %gather_fusion = bf16[256,128]{1,0:T(8,128)(2,1)S(1)} fusion(bf16[32768,128]{1,0:T(8,128)(2,1)} %table.1, s32[1024]{0:T(1024)S(1)} %pad_clamp_fusion), kind=kCustom, calls=%fused_computation | custom fusion | bytes 132096 | tf_op jit(solution)/shard_map/jit(_take)/gather | solution.py:374
  15.2 0.1 broadcast_select_fusion
  15.3 35.2 %all_gather.3 = bf16[256,1024]{1,0:T(8,128)(2,1)S(1)} all-gather(bf16[256,128]{1,0:T(8,128)(2,1)S(1)} %broadcast_select_fusion), channel_id=1, replica_groups=mesh['col'=8,'req'=64] {'col'}, dimensions={1}, use_global_device_ids=true | all-gather | bytes 589824 | tf_op jit(solution)/shard_map/all_gather | solution.py:376
  50.5 0.0 copy-done
  50.5 0.3 fusion.13
  50.9 0.0 copy-start.1
  50.9 1.0 copy-done.1
  51.9 0.0 copy-start.2
  51.9 220.2 %attend_chunk.1 = f32[256,128]{1,0:T(8,128)S(1)} custom-call(bf16[32768,128]{1,0:T(8,128)(2,1)} %table.1, bf16[1024,256]{1,0:T(8,128)(2,1)S(1)} %copy-done.1, bf16[256,128]{1,0:T(8,128)(2,1)S(1)} %slice.16.q_in, f32[16,16,256]{2,1,0:T(8,128)S(1)} %pad_maximum_fusion.msg_in), custom_call_target="tpu_custom_call" | custom-call | flops 7516192768 | bytes 4194304 | tf_op jit(solution)/shard_map/attend_chunk/pallas_call | solution.py:334
  272.2 0.1 fusion.12
  272.3 17.6 %all-reduce = (f32[256]{0:T(256)S(1)}, f32[256]{0:T(256)S(1)}) all-reduce(f32[256]{0:T(256)S(1)} %get-tuple-element.6, f32[256]{0:T(256)S(1)} %get-tuple-element.5), channel_id=1, replica_groups=mesh['col'=8,'req'=64] {'col'}, use_global_device_ids=true, to_apply=%region_3.4 | all-reduce | flops 512 | bytes 4096 | tf_op jit(solution)/shard_map/psum | solution.py:394
  289.9 0.0 copy-done.2
  289.9 1.3 convolution_bitcast_fusion
  291.2 0.0 reduce-scatter.2.cloned.1.call-update
  291.3 53.3 %reduce-scatter.2.cloned.1.call-done = f32[128,256]{0,1:T(8,128)} async-done(((f32[1024,256]{0,1:T(8,128)}), f32[128,256]{0,1:T(8,128)}) %reduce-scatter.2.cloned.1.call-update) | async-done | bytes 131088 | tf_op jit(solution)/shard_map/reduce_scatter | solution.py:399
  344.6 1.6 fusion.3
  (6 shorter events, 0.1 us)
Async XLA Ops:
  6.5 44.0 %copy-start = (bf16[1024,256]{1,0:T(8,128)(2,1)S(1)}, bf16[1024,256]{1,0:T(8,128)(2,1)}, u32[]{:S(2)}) copy-start(bf16[1024,256]{1,0:T(8,128)(2,1)} %param.12) | copy-start | bytes 1572868
  6.5 338.0 %reduce-scatter.2.cloned.1.call-start = ((), (), s32[]{:S(2)}) async-start(), calls=%async_computation.1 | async-start | bytes 1179648 | tf_op jit(solution)/shard_map/reduce_scatter | solution.py:399
  50.9 1.0 copy-start.1
  51.9 238.0 %copy-start.2 = (bf16[128,1024]{1,0:T(8,128)(2,1)S(1)}, bf16[128,1024]{1,0:T(8,128)(2,1)}, u32[]{:S(2)}) copy-start(bf16[128,1024]{1,0:T(8,128)(2,1)} %param.13) | copy-start | bytes 786436
Sparse Core Ops, SparseCore 0:
  291.4 53.1 reduce-scatter.1

commit v2 on v1

v2 whole, which is shorter than its diff:
```python
import functools
import math

import jax
import jax.numpy as jnp
from jax import lax
from jax.experimental import pallas as pl
from jax.experimental.pallas import tpu as pltpu
from jax.sharding import PartitionSpec as P

D = 1024
DH = 128
GROUP = 16
HIST = 2048
REQ_GROUP = 16
CHUNK = 2048
CAND = 256
PIECES = 8
ROWS = CHUNK // PIECES
LAG = 2
CAND_STEP = 6
PAIR = 2 * CAND
TILE = 512
MESH = pl.DeviceIdType.MESH
NT = (((1,), (1,)), ((), ()))


def layer_kernel(
    table, w_kv, w_qu, w_out, cand_in, msg_in, out,
    rows, cands, keys, values, queries, msgs, counts, onehot, gate, parts_out, parts_in, own_part,
    moments, shares, share_out, share_near, share_in,
    own_sem, ring_send, ring_recv, pair_send, pair_recv, c_send, c_recv, cp_send, cp_recv,
    q_send, q_recv, m_send, m_recv, p_send, p_recv, s_send, s_recv, o_send, o_recv,
    x_send, x_recv, local_sem,
):
    col, req = lax.axis_index("col"), lax.axis_index("req")
    z_hi, core = col // 2, col % 2
    z_lo, me = req // 16, req % 16
    z = z_hi * 4 + z_lo

    def at_z(other):
        other = lax.rem(other + 16, 16)
        return (other // 4 * 2 + core, other % 4 * 16 + me)

    above, below = at_z(z + 1), at_z(z - 1)
    sibling = (z_hi * 2 + 1 - core, req)
    mine = pl.ds(pl.multiple_of(me * CAND, CAND), CAND)
    below_block, above_block = lax.rem(z_hi + 3, 4), lax.rem(z_hi + 1, 4)
    far_block = lax.rem(z_hi + 2, 4)

    def peer(index):
        return (col, z_lo * 16 + index)

    def column(block):
        return (block * 2 + core, req)

    def remote(src, dst, sent, arrived, target):
        return pltpu.make_async_remote_copy(
            src_ref=src,
            dst_ref=dst,
            send_sem=sent,
            recv_sem=arrived,
            device_id=target,
            device_id_type=MESH,
        )

    barrier = pltpu.get_barrier_semaphore()
    for other in (above, below):
        pl.semaphore_signal(barrier, inc=1, device_id=other, device_id_type=MESH)

    def greet(j, carry):
        pl.semaphore_signal(
            barrier, inc=1, device_id=peer(lax.rem(me + j, 16)), device_id_type=MESH
        )
        return carry

    lax.fori_loop(1, 16, greet, 0)

    def greet_column(j, carry):
        pl.semaphore_signal(
            barrier, inc=1, device_id=(lax.rem(col + j, 8), req), device_id_type=MESH
        )
        return carry

    lax.fori_loop(1, 8, greet_column, 0)

    def place(block, half, p):
        return rows.at[block * 2 + half, pl.ds(pl.multiple_of(p * ROWS, ROWS), ROWS), :]

    def own_copy(p):
        start = pl.multiple_of(me * CHUNK + p * ROWS, ROWS)
        return pltpu.make_async_copy(
            table.at[pl.ds(start, ROWS), :], place(z_hi, core, p), own_sem.at[p]
        )

    for p in range(PIECES):
        own_copy(p).start()
    m_own = pltpu.make_async_copy(msg_in.at[me], msgs.at[me], local_sem.at[0])
    m_own.start()
    cands[col] = cand_in[...]
    pl.semaphore_wait(barrier, 24)

    def cand_copy(block, target, kind):
        slot = cands.at[block * 2 + core]
        return remote(slot, slot, c_send.at[kind], c_recv.at[kind], column(target))

    cand_copy(z_hi, above_block, 0).start()
    cand_copy(z_hi, below_block, 1).start()
    cand_copy(z_hi, far_block, 2).start()

    def cand_across(block, slot):
        ref = cands.at[block * 2 + core]
        return remote(ref, ref, cp_send.at[slot], cp_recv.at[slot], sibling)

    cand_across(z_hi, 0).start()

    def ring(block, p, target, kind):
        ref = place(block, core, p)
        return remote(ref, ref, ring_send.at[kind, p], ring_recv.at[kind, p], target)

    def across(block, p, slot):
        ref = place(block, core, p)
        return remote(ref, ref, pair_send.at[slot, p], pair_recv.at[slot, p], sibling)

    def send_own(p, carry):
        own_copy(p).wait()

        @pl.when(z_lo == 3)
        def _():
            ring(z_hi, p, above, 0).start()

        @pl.when(z_lo == 0)
        def _():
            ring(z_hi, p, below, 1).start()

        across(z_hi, p, 0).start()
        return carry

    lax.fori_loop(0, PIECES, send_own, 0)

    def m_copy(j, slot):
        to = lax.rem(me + j, 16)
        return remote(msg_in.at[to], msgs.at[slot], m_send.at[j], m_recv.at[slot], peer(to))

    def q_copy(j, slot):
        to = lax.rem(me + j, 16)
        part = queries.at[pl.ds(pl.multiple_of(slot * CAND, CAND), CAND), :]
        return remote(part, part, q_send.at[j], q_recv.at[slot], peer(to))

    def spread_m(j, carry):
        m_copy(j, me).start()
        return carry

    def spread_q(j, carry):
        q_copy(j, me).start()
        return carry

    lax.fori_loop(1, 16, spread_m, 0)

    up_lag, down_lag = LAG * z_lo, LAG * (3 - z_lo)

    def ring_step(t, carry):
        p = t - up_lag

        @pl.when((p >= 0) & (p < PIECES))
        def _():
            ring(below_block, p, below, 0).wait_recv()

            @pl.when(z_lo < 3)
            def _():
                ring(below_block, p, above, 0).start()

            @pl.when((z_lo == 3) & (lax.rem(p, 2) == 0))
            def _():
                ring(below_block, p, above, 2).start()

            across(below_block, p, 1).start()

        p1 = t - down_lag

        @pl.when((p1 >= 0) & (p1 < PIECES))
        def _():
            ring(above_block, p1, above, 1).wait_recv()

            @pl.when(z_lo > 0)
            def _():
                ring(above_block, p1, below, 1).start()

            @pl.when((z_lo == 0) & (lax.rem(p1, 2) == 1))
            def _():
                ring(above_block, p1, below, 2).start()

            across(above_block, p1, 2).start()

        p2 = t - up_lag - 4 * LAG

        @pl.when((p2 >= 0) & (p2 < PIECES) & (lax.rem(p2 + 32, 2) == 0))
        def _():
            ring(far_block, p2, below, 2).wait_recv()

            @pl.when(z_lo < 3)
            def _():
                ring(far_block, p2, above, 2).start()

            across(far_block, p2, 3).start()

        p3 = t - down_lag - 4 * LAG

        @pl.when((p3 >= 0) & (p3 < PIECES) & (lax.rem(p3 + 32, 2) == 1))
        def _():
            ring(far_block, p3, above, 2).wait_recv()

            @pl.when(z_lo > 0)
            def _():
                ring(far_block, p3, below, 2).start()

            across(far_block, p3, 3).start()

        @pl.when(t == CAND_STEP)
        def _():
            cand_copy(below_block, below_block, 0).wait_recv()
            cand_across(below_block, 1).start()
            cand_copy(above_block, above_block, 1).wait_recv()
            cand_across(above_block, 2).start()
            cand_copy(far_block, far_block, 2).wait_recv()
            cand_across(far_block, 3).start()

        @pl.when(t == CAND_STEP + 1)
        def _():
            for slot in range(4):
                cand_across(z_hi, slot).wait_recv()
            joined = jnp.concatenate([cands[k] for k in range(8)], 1)
            both = jnp.dot(joined, w_qu[...], preferred_element_type=jnp.float32)
            queries[mine, :] = both[:, :DH].astype(jnp.bfloat16)
            gate[...] = both[:, DH:]
            lax.fori_loop(1, 16, spread_q, 0)

        p4 = t - 7 * LAG - 1

        @pl.when((p4 >= 0) & (p4 < PIECES))
        def _():
            for slot in range(4):
                across(z_hi, p4, slot).wait_recv()
            here = pl.ds(pl.multiple_of(p4 * ROWS, ROWS), ROWS)
            joined = jnp.concatenate([rows[k, here, :] for k in range(8)], 1)
            both = jnp.dot(joined, w_kv[...], preferred_element_type=jnp.float32)
            both = both.astype(jnp.bfloat16)
            keys[here, :] = both[:, :DH]
            values[here, :] = both[:, DH:]

        return carry

    lax.fori_loop(0, PIECES + 7 * LAG + 1, ring_step, 0)

    m_own.wait()

    def arrived(j, carry):
        src = lax.rem(me + j, 16)
        m_copy(j, src).wait_recv()
        q_copy(j, src).wait_recv()
        return carry

    lax.fori_loop(1, 16, arrived, 0)
    for s in range(8):
        count = msgs[:, s, :]
        high = jnp.floor(count * (1.0 / 256.0))
        low = count - high * 256.0
        counts[:, s * 256 : (s + 1) * 256] = jnp.concatenate(
            [low, high, jnp.zeros((96, 256), jnp.float32)], 0
        ).astype(jnp.bfloat16)

    def mark(src, carry):
        wanted = msgs[src, 8:9, :]
        lane = lax.broadcasted_iota(jnp.int32, (DH, CAND), 0).astype(jnp.float32)
        hot = jnp.where(lane == wanted, 1.0, 0.0) + jnp.where(lane == wanted + 16.0, 256.0, 0.0)
        onehot[pl.ds(pl.multiple_of(src * CAND, CAND), CAND), :] = hot.T.astype(jnp.bfloat16)
        return carry

    lax.fori_loop(0, 16, mark, 0)

    half_scale = 0.5 / math.sqrt(DH)

    def part_copy(to, slot):
        return remote(parts_out.at[to], parts_in.at[slot], p_send.at[to], p_recv.at[slot], peer(to))

    def attend_pair(i, carry):
        pair = lax.rem(me // 2 + 1 + i, 8)
        here = pl.ds(pl.multiple_of(pair * PAIR, PAIR), PAIR)
        picked, hot = queries[here, :], onehot[here, :]
        total = jnp.zeros((PAIR, DH), jnp.float32)
        for r in range(CHUNK // TILE):
            span = slice(r * TILE, (r + 1) * TILE)
            u = lax.dot_general(picked, keys[span, :], NT, preferred_element_type=jnp.float32)
            times = jnp.dot(hot, counts[:, span], preferred_element_type=jnp.float32)
            u = u * half_scale
            weight = ((u + u * jnp.tanh(u)) * times).astype(jnp.bfloat16)
            total += jnp.dot(weight, values[span, :], preferred_element_type=jnp.float32)
        for k in range(2):
            src = pair * 2 + k
            part = total[k * CAND : (k + 1) * CAND]

            @pl.when(src == me)
            def _():
                own_part[...] = part

            @pl.when(src != me)
            def _():
                parts_out[src] = part.astype(jnp.bfloat16)
                part_copy(src, me).start()

        return carry

    lax.fori_loop(0, 8, attend_pair, 0)

    def collect(j, carry):
        src = lax.rem(me + j, 16)
        part_copy(src, src).wait_recv()
        own_part[...] += parts_in[src].astype(jnp.float32)
        return carry

    lax.fori_loop(1, 16, collect, 0)

    attended = (own_part[...] * (1.0 / HIST)).T
    moments[col, 0:1, :] = jnp.sum(attended, axis=0, keepdims=True)
    moments[col, 1:2, :] = jnp.sum(attended * attended, axis=0, keepdims=True)
    moments[col, 2:8, :] = jnp.zeros((6, CAND), jnp.float32)

    def moment_copy(j, slot):
        ref = moments.at[slot]
        return remote(ref, ref, s_send.at[j], s_recv.at[slot], (lax.rem(col + j, 8), req))

    def spread_moments(j, carry):
        moment_copy(j, col).start()
        return carry

    lax.fori_loop(1, 8, spread_moments, 0)
    gate_t = gate[...].T
    gate_t = gate_t / (1.0 + jnp.exp(-gate_t))

    def moments_arrived(j, carry):
        moment_copy(j, lax.rem(col + j, 8)).wait_recv()
        return carry

    lax.fori_loop(1, 8, moments_arrived, 0)
    summed = moments[0]
    for k in range(1, 8):
        summed = summed + moments[k]
    average = summed[0:1, :] * (1.0 / D)
    variance = summed[1:2, :] * (1.0 / D) - average * average
    gated = ((attended - average) * lax.rsqrt(variance + 1e-05) * gate_t).T.astype(jnp.bfloat16)

    product = jnp.dot(gated, w_out[...], preferred_element_type=jnp.float32)
    for k in range(8):
        shares[k] = product[:, k * 128 : (k + 1) * 128]

    def share_across(block):
        return remote(
            shares.at[block * 2 + 1 - core], share_near.at[block], x_send.at[block], x_recv.at[block],
            sibling,
        )

    def share_copy(block, kind):
        return remote(
            share_out.at[kind], share_in.at[kind], o_send.at[kind], o_recv.at[kind], column(block)
        )

    order = ((far_block, 2), (above_block, 0), (below_block, 1))
    for block, _ in order + ((z_hi, 3),):
        share_across(block).start()
    for block, kind in order:
        share_across(block).wait_recv()
        share_out[kind] = (shares[block * 2 + core] + share_near[block]).astype(jnp.bfloat16)
        share_copy(block, kind).start()
    share_across(z_hi).wait_recv()
    own_part[...] = shares[col] + share_near[z_hi] + cand_in[...].astype(jnp.float32)
    for kind in (0, 1, 2):
        share_copy(z_hi, kind).wait_recv()
        own_part[...] += share_in[kind].astype(jnp.float32)
    out[...] = own_part[...].astype(jnp.bfloat16)

    def sent_ring(p, carry):
        for kind in range(3):
            ring(far_block, p, above, kind).wait_send()
        for slot in range(4):
            across(far_block, p, slot).wait_send()
        return carry

    lax.fori_loop(0, PIECES, sent_ring, 0)

    def sent_plane(j, carry):
        m_copy(j, me).wait_send()
        q_copy(j, me).wait_send()
        part_copy(lax.rem(me + j, 16), me).wait_send()
        return carry

    lax.fori_loop(1, 16, sent_plane, 0)

    def sent_moments(j, carry):
        moment_copy(j, col).wait_send()
        return carry

    lax.fori_loop(1, 8, sent_moments, 0)
    for kind in range(3):
        cand_copy(z_hi, far_block, kind).wait_send()
        share_copy(z_hi, kind).wait_send()
    for slot in range(4):
        cand_across(z_hi, slot).wait_send()
        share_across(slot).wait_send()


def layer(table, w_kv, w_qu, w_out, cand_slice, msg):
    vmem = pl.BlockSpec(memory_space=pltpu.VMEM)
    dma = pltpu.SemaphoreType.DMA
    bf16, f32 = jnp.bfloat16, jnp.float32
    return pl.pallas_call(
        layer_kernel,
        out_shape=jax.ShapeDtypeStruct((CAND, DH), bf16),
        in_specs=[pl.BlockSpec(memory_space=pl.ANY)] + [vmem] * 5,
        out_specs=vmem,
        scratch_shapes=[
            pltpu.VMEM((8, CHUNK, 128), bf16),
            pltpu.VMEM((8, CAND, 128), bf16),
            pltpu.VMEM((CHUNK, DH), bf16),
            pltpu.VMEM((CHUNK, DH), bf16),
            pltpu.VMEM((16 * CAND, DH), bf16),
            pltpu.VMEM((16, 16, CAND), f32),
            pltpu.VMEM((DH, CHUNK), bf16),
            pltpu.VMEM((16 * CAND, DH), bf16),
            pltpu.VMEM((CAND, DH), f32),
            pltpu.VMEM((16, CAND, DH), bf16),
            pltpu.VMEM((16, CAND, DH), bf16),
            pltpu.VMEM((CAND, DH), f32),
            pltpu.VMEM((8, 8, CAND), f32),
            pltpu.VMEM((8, CAND, 128), f32),
            pltpu.VMEM((3, CAND, 128), bf16),
            pltpu.VMEM((4, CAND, 128), f32),
            pltpu.VMEM((3, CAND, 128), bf16),
            dma((PIECES,)),
            dma((3, PIECES)),
            dma((3, PIECES)),
            dma((4, PIECES)),
            dma((4, PIECES)),
            dma((3,)),
            dma((3,)),
            dma((4,)),
            dma((4,)),
            dma((16,)),
            dma((16,)),
            dma((16,)),
            dma((16,)),
            dma((16,)),
            dma((16,)),
            dma((8,)),
            dma((8,)),
            dma((3,)),
            dma((3,)),
            dma((4,)),
            dma((4,)),
            dma((1,)),
        ],
        compiler_params=pltpu.CompilerParams(
            collective_id=0, has_side_effects=True, vmem_limit_bytes=48 << 20
        ),
        cost_estimate=pl.CostEstimate(
            flops=8 << 30, bytes_accessed=4 << 20, transcendentals=8 << 20
        ),
        name="layer",
    )(table, w_kv, w_qu, w_out, cand_slice, msg)


def on_device(event_ids, cand_ids, cand_request, table, w_kv, w_qu, w_out):
    cand_slice = jnp.take(table, cand_ids, axis=0)
    high = (event_ids[None, :] // 128 == jnp.arange(256, dtype=jnp.int32)[:, None]).astype(
        jnp.bfloat16
    )
    low = (event_ids[None, :] % 128 == jnp.arange(128, dtype=jnp.int32)[:, None]).astype(
        jnp.bfloat16
    )
    times = lax.dot_general(high, low, NT, preferred_element_type=jnp.float32)
    wanted = (cand_request % REQ_GROUP).astype(jnp.float32)
    msg = jnp.concatenate(
        [times.reshape(16, 8, 256), jnp.broadcast_to(wanted[None, None, :], (16, 8, 256))], 1
    )
    return layer(table, w_kv, w_qu, w_out, cand_slice, msg)


def solution(mesh):
    in_specs = (
        P("req"),
        P("req"),
        P("req"),
        P(None, "col"),
        P(None, "col"),
        P(None, "col"),
        P("col", None),
    )
    out_specs = P("req", "col")
    return jax.shard_map(
        on_device, mesh=mesh, in_specs=in_specs, out_specs=out_specs, check_vma=False
    )
```

time: 356 us -> 130 us (0.37)
  Pallas kernels: 220 us -> 117 us
  waiting for transfers between devices: 53.3 us -> 0 us
  blocking collectives: 52.8 us -> 0 us
  between operations: 13.5 us -> 0.05 us
    pallas_call x1, Pallas kernels: 220 us -> 117 us  [layer(): pl.pallas_call(layer_kernel, out_shape=jax.ShapeDtypeStruct((CAND, DH), b...]
    reduce_scatter x1 -> x0, waiting for transfers between devices: 53.3 us -> none  [on_device(): lax.psum_scatter(lax.dot_general(w_out, gated, (((0,), (1,)), ((), ())),...]
    all_gather x1 -> x0, blocking collectives: 35.2 us -> none  [on_device(): lax.all_gather(cand_slice, 'col', axis=1, tiled=True)]
    psum x1 -> x0, blocking collectives: 17.6 us -> none  [on_device(): lax.psum((jnp.sum(features, 1), jnp.sum(features * features, 1)), 'col')]
  transfers between devices with their start and end apart: 1 -> 0, of which waited for: 1 -> 0; matrix products, arithmetic and copies ran while one was open for 0% -> 0% of each run, Pallas kernels for 0% -> 0%
where the time goes in v2:
time: 130 us
  Pallas kernels  117 us (90%)
  local copies, waits for them, and re-layouts  8.9 us (7%)
  other arithmetic  2.9 us (2%)
    pallas_call x1, Pallas kernels, layer(): pl.pallas_call(layer_kernel, out_shape=jax.ShapeDtypeStruct((CAND, DH), b...  117 us
    gather x1, local copies, waits for them, and re-layouts, on_device(): cand_slice = jnp.take(table, cand_ids, axis=0)  5.19 us
    unnamed x7, local copies, waits for them, and re-layouts  3.66 us

profile of v2, /device:TPU:1, one launch (start us, length us, event | category | flops | bytes accessed | tf_op | source)
XLA Modules:
  0.0 129.6 jit_solution(323652605718084055)
XLA Ops:
  0.0 0.7 add_select_fusion
  0.7 0.5 fusion
  1.3 0.7 fusion.5
  2.0 0.7 compare_select_fusion
  2.7 5.2 %gather_fusion = bf16[256,128]{1,0:T(8,128)(2,1)S(1)} fusion(bf16[32768,128]{1,0:T(8,128)(2,1)} %table.1, s32[1024]{0:T(1024)S(1)} %pad_clamp_fusion), kind=kCustom, calls=%fused_computation | custom fusion | bytes 132096 | tf_op jit(solution)/shard_map/jit(_take)/gather | solution.py:472
  7.9 0.7 compare_and_fusion
  8.6 0.1 broadcast_select_fusion.cand_in
  8.7 0.0 copy-start
  8.7 1.0 copy-done
  9.8 0.0 copy-start.1
  9.8 1.0 copy-done.1
  10.8 0.0 copy-start.2
  10.8 0.9 copy-done.2
  11.8 117.2 %layer.1 = bf16[256,128]{1,0:T(8,128)(2,1)S(1)} custom-call(bf16[32768,128]{1,0:T(8,128)(2,1)} %table.1, bf16[1024,256]{1,0:T(8,128)(2,1)S(1)} %copy-done, bf16[1024,256]{1,0:T(8,128)(2,1)S(1)} %copy-done.1, bf16[128,1024]{1,0:T(8,128)(2,1)S(1)} %copy-done.2, bf16[256,128]{1,0:T(8,128)(2,1)S(1)} %broadcast_select_fusion.cand_in, ...), custom_call_target="tpu_custom_call" | custom-call | flops 8589934592 | bytes 4194304 | tf_op jit(solution)/shard_map/layer/pallas_call | solution.py:415
  129.0 0.6 copy.9
  (4 shorter events, 0.1 us)
Async XLA Ops:
  8.7 1.0 copy-start
  9.8 1.0 copy-start.1
  10.8 0.9 copy-start.2

commit v3 on v2

--- a/solution.py
+++ b/solution.py
@@ -18,7 +18,8 @@
 PIECES = 8
 ROWS = CHUNK // PIECES
 LAG = 2
-CAND_STEP = 6
+CAND_STEP = 3
+FAR_STEP = 5
 PAIR = 2 * CAND
 TILE = 512
 MESH = pl.DeviceIdType.MESH
@@ -26,8 +27,8 @@
 
 
 def layer_kernel(
-    table, w_kv, w_qu, w_out, cand_in, msg_in, out,
-    rows, cands, keys, values, queries, msgs, counts, onehot, gate, parts_out, parts_in, own_part,
+    events, cand_ids, cand_row, wanted_in, table, table_tiles, w_kv_in, w_qu_in, w_out_in, out,
+    table_here, w_kv, w_qu, w_out, msg_out, within, rows, cands, keys, values, queries, msgs, counts, onehot, gate, parts_out, parts_in, own_part,
     moments, shares, share_out, share_near, share_in,
     own_sem, ring_send, ring_recv, pair_send, pair_recv, c_send, c_recv, cp_send, cp_recv,
     q_send, q_recv, m_send, m_recv, p_send, p_recv, s_send, s_recv, o_send, o_recv,
@@ -95,9 +96,30 @@
 
     for p in range(PIECES):
         own_copy(p).start()
-    m_own = pltpu.make_async_copy(msg_in.at[me], msgs.at[me], local_sem.at[0])
-    m_own.start()
-    cands[col] = cand_in[...]
+    table_copy = pltpu.make_async_copy(table_tiles, table_here, local_sem.at[0])
+    kv_copy = pltpu.make_async_copy(w_kv_in, w_kv, local_sem.at[1])
+    qu_copy = pltpu.make_async_copy(w_qu_in, w_qu, local_sem.at[2])
+    out_copy = pltpu.make_async_copy(w_out_in, w_out, local_sem.at[3])
+    for copy in (table_copy, qu_copy, kv_copy, out_copy):
+        copy.start()
+
+    place_in = (cand_row[...] & 15).astype(jnp.float32)
+    within[...] = jnp.broadcast_to(place_in, (128, CAND)).T
+    lane = lax.broadcasted_iota(jnp.int32, (16, 256), 1)
+    lane = (lane - 16 * lax.broadcasted_iota(jnp.int32, (16, 256), 0)).astype(jnp.float32)
+    table_copy.wait()
+
+    def look_up(g, carry):
+        for k in range(4):
+            first = pl.multiple_of(g * 64 + k * 16, 16)
+            tiles = [table_here[cand_ids[first + i] >> 4] for i in range(16)]
+            wide = within[pl.ds(first, 16), :]
+            pick = jnp.where(lane == jnp.concatenate([wide, wide], 1), 1.0, 0.0).astype(jnp.bfloat16)
+            found = jnp.dot(pick, jnp.concatenate(tiles, 0), preferred_element_type=jnp.float32)
+            cands[col, pl.ds(first, 16), :] = found.astype(jnp.bfloat16)
+        return carry
+
+    lax.fori_loop(0, 4, look_up, 0)
     pl.semaphore_wait(barrier, 24)
 
     def cand_copy(block, target, kind):
@@ -122,25 +144,51 @@
         ref = place(block, core, p)
         return remote(ref, ref, pair_send.at[slot, p], pair_recv.at[slot, p], sibling)
 
-    def send_own(p, carry):
+    half = PIECES // 2
+
+    def in_turn(i, first):
+        return jnp.where(i < half, 2 * i + first, 2 * (i - half) + 1 - first)
+
+    def own_here(p, carry):
         own_copy(p).wait()
-
+        across(z_hi, p, 0).start()
+        return carry
+
+    def send_own(i, carry):
         @pl.when(z_lo == 3)
         def _():
-            ring(z_hi, p, above, 0).start()
+            ring(z_hi, in_turn(i, 0), above, 0).start()
 
         @pl.when(z_lo == 0)
         def _():
-            ring(z_hi, p, below, 1).start()
-
-        across(z_hi, p, 0).start()
-        return carry
-
+            ring(z_hi, in_turn(i, 1), below, 1).start()
+
+        return carry
+
+    lax.fori_loop(0, PIECES, own_here, 0)
     lax.fori_loop(0, PIECES, send_own, 0)
+
+    times = jnp.zeros((256, 128), jnp.float32)
+    for k in range(4):
+        some = events[:, k * 512 : (k + 1) * 512]
+        high = lax.broadcasted_iota(jnp.int32, (256, 512), 0) == some // 128
+        low = lax.broadcasted_iota(jnp.int32, (128, 512), 0) == some % 128
+        times += lax.dot_general(
+            jnp.where(high, 1.0, 0.0).astype(jnp.bfloat16),
+            jnp.where(low, 1.0, 0.0).astype(jnp.bfloat16),
+            NT,
+            preferred_element_type=jnp.float32,
+        )
+    wanted_here = (wanted_in[...] % REQ_GROUP).astype(jnp.float32)
+    for k in range(16):
+        msg_out[k, 0:16, :] = times[k * 16 : (k + 1) * 16]
+        msg_out[k, 16:18, :] = wanted_here
+        msg_out[k, 18:24, :] = jnp.zeros((6, 128), jnp.float32)
+    msgs[me] = msg_out[me]
 
     def m_copy(j, slot):
         to = lax.rem(me + j, 16)
-        return remote(msg_in.at[to], msgs.at[slot], m_send.at[j], m_recv.at[slot], peer(to))
+        return remote(msg_out.at[to], msgs.at[slot], m_send.at[j], m_recv.at[slot], peer(to))
 
     def q_copy(j, slot):
         to = lax.rem(me + j, 16)
@@ -160,61 +208,65 @@
     up_lag, down_lag = LAG * z_lo, LAG * (3 - z_lo)
 
     def ring_step(t, carry):
-        p = t - up_lag
-
-        @pl.when((p >= 0) & (p < PIECES))
-        def _():
+        i0 = t - up_lag
+
+        @pl.when((i0 >= 0) & (i0 < PIECES))
+        def _():
+            p = in_turn(i0, 0)
             ring(below_block, p, below, 0).wait_recv()
 
             @pl.when(z_lo < 3)
             def _():
                 ring(below_block, p, above, 0).start()
 
-            @pl.when((z_lo == 3) & (lax.rem(p, 2) == 0))
+            @pl.when((z_lo == 3) & (i0 < half))
             def _():
                 ring(below_block, p, above, 2).start()
 
             across(below_block, p, 1).start()
 
-        p1 = t - down_lag
-
-        @pl.when((p1 >= 0) & (p1 < PIECES))
-        def _():
-            ring(above_block, p1, above, 1).wait_recv()
+        i1 = t - down_lag
+
+        @pl.when((i1 >= 0) & (i1 < PIECES))
+        def _():
+            p = in_turn(i1, 1)
+            ring(above_block, p, above, 1).wait_recv()
 
             @pl.when(z_lo > 0)
             def _():
-                ring(above_block, p1, below, 1).start()
-
-            @pl.when((z_lo == 0) & (lax.rem(p1, 2) == 1))
-            def _():
-                ring(above_block, p1, below, 2).start()
-
-            across(above_block, p1, 2).start()
-
-        p2 = t - up_lag - 4 * LAG
-
-        @pl.when((p2 >= 0) & (p2 < PIECES) & (lax.rem(p2 + 32, 2) == 0))
-        def _():
-            ring(far_block, p2, below, 2).wait_recv()
+                ring(above_block, p, below, 1).start()
+
+            @pl.when((z_lo == 0) & (i1 < half))
+            def _():
+                ring(above_block, p, below, 2).start()
+
+            across(above_block, p, 2).start()
+
+        i2 = t - up_lag - 4 * LAG
+
+        @pl.when((i2 >= 0) & (i2 < half))
+        def _():
+            p = 2 * i2
+            ring(far_block, p, below, 2).wait_recv()
 
             @pl.when(z_lo < 3)
             def _():
-                ring(far_block, p2, above, 2).start()
-
-            across(far_block, p2, 3).start()
-
-        p3 = t - down_lag - 4 * LAG
-
-        @pl.when((p3 >= 0) & (p3 < PIECES) & (lax.rem(p3 + 32, 2) == 1))
-        def _():
-            ring(far_block, p3, above, 2).wait_recv()
+                ring(far_block, p, above, 2).start()
+
+            across(far_block, p, 3).start()
+
+        i3 = t - down_lag - 4 * LAG
+
+        @pl.when((i3 >= 0) & (i3 < half))
+        def _():
+            p = 2 * i3 + 1
+            ring(far_block, p, above, 2).wait_recv()
 
             @pl.when(z_lo > 0)
             def _():
-                ring(far_block, p3, below, 2).start()
-
-            across(far_block, p3, 3).start()
+                ring(far_block, p, below, 2).start()
+
+            across(far_block, p, 3).start()
 
         @pl.when(t == CAND_STEP)
         def _():
@@ -222,26 +274,31 @@
             cand_across(below_block, 1).start()
             cand_copy(above_block, above_block, 1).wait_recv()
             cand_across(above_block, 2).start()
+
+        @pl.when(t == FAR_STEP)
+        def _():
             cand_copy(far_block, far_block, 2).wait_recv()
             cand_across(far_block, 3).start()
 
-        @pl.when(t == CAND_STEP + 1)
+        @pl.when(t == FAR_STEP + 1)
         def _():
             for slot in range(4):
                 cand_across(z_hi, slot).wait_recv()
+            qu_copy.wait()
             joined = jnp.concatenate([cands[k] for k in range(8)], 1)
             both = jnp.dot(joined, w_qu[...], preferred_element_type=jnp.float32)
             queries[mine, :] = both[:, :DH].astype(jnp.bfloat16)
             gate[...] = both[:, DH:]
             lax.fori_loop(1, 16, spread_q, 0)
 
-        p4 = t - 7 * LAG - 1
-
-        @pl.when((p4 >= 0) & (p4 < PIECES))
+        i4 = t - 7 * LAG - 1
+
+        @pl.when((i4 >= 0) & (i4 < half))
         def _():
             for slot in range(4):
-                across(z_hi, p4, slot).wait_recv()
-            here = pl.ds(pl.multiple_of(p4 * ROWS, ROWS), ROWS)
+                across(z_hi, 2 * i4, slot).wait_recv()
+                across(z_hi, 2 * i4 + 1, slot).wait_recv()
+            here = pl.ds(pl.multiple_of(i4 * 2 * ROWS, 2 * ROWS), 2 * ROWS)
             joined = jnp.concatenate([rows[k, here, :] for k in range(8)], 1)
             both = jnp.dot(joined, w_kv[...], preferred_element_type=jnp.float32)
             both = both.astype(jnp.bfloat16)
@@ -250,9 +307,8 @@
 
         return carry
 
-    lax.fori_loop(0, PIECES + 7 * LAG + 1, ring_step, 0)
-
-    m_own.wait()
+    kv_copy.wait()
+    lax.fori_loop(0, PIECES // 2 + 7 * LAG + 1, ring_step, 0)
 
     def arrived(j, carry):
         src = lax.rem(me + j, 16)
@@ -261,19 +317,21 @@
         return carry
 
     lax.fori_loop(1, 16, arrived, 0)
-    for s in range(8):
+    for s in range(16):
         count = msgs[:, s, :]
         high = jnp.floor(count * (1.0 / 256.0))
         low = count - high * 256.0
-        counts[:, s * 256 : (s + 1) * 256] = jnp.concatenate(
-            [low, high, jnp.zeros((96, 256), jnp.float32)], 0
+        counts[:, s * 128 : (s + 1) * 128] = jnp.concatenate(
+            [low, high, jnp.zeros((96, 128), jnp.float32)], 0
         ).astype(jnp.bfloat16)
 
     def mark(src, carry):
-        wanted = msgs[src, 8:9, :]
-        lane = lax.broadcasted_iota(jnp.int32, (DH, CAND), 0).astype(jnp.float32)
-        hot = jnp.where(lane == wanted, 1.0, 0.0) + jnp.where(lane == wanted + 16.0, 256.0, 0.0)
-        onehot[pl.ds(pl.multiple_of(src * CAND, CAND), CAND), :] = hot.T.astype(jnp.bfloat16)
+        lane = lax.broadcasted_iota(jnp.int32, (DH, 128), 0).astype(jnp.float32)
+        for k in range(2):
+            wanted = msgs[src, 16 + k : 17 + k, :]
+            hot = jnp.where(lane == wanted, 1.0, 0.0) + jnp.where(lane == wanted + 16.0, 256.0, 0.0)
+            start = pl.multiple_of(src * CAND + k * 128, 128)
+            onehot[pl.ds(start, 128), :] = hot.T.astype(jnp.bfloat16)
         return carry
 
     lax.fori_loop(0, 16, mark, 0)
@@ -349,6 +407,7 @@
     variance = summed[1:2, :] * (1.0 / D) - average * average
     gated = ((attended - average) * lax.rsqrt(variance + 1e-05) * gate_t).T.astype(jnp.bfloat16)
 
+    out_copy.wait()
     product = jnp.dot(gated, w_out[...], preferred_element_type=jnp.float32)
     for k in range(8):
         shares[k] = product[:, k * 128 : (k + 1) * 128]
@@ -372,7 +431,7 @@
         share_out[kind] = (shares[block * 2 + core] + share_near[block]).astype(jnp.bfloat16)
         share_copy(block, kind).start()
     share_across(z_hi).wait_recv()
-    own_part[...] = shares[col] + share_near[z_hi] + cand_in[...].astype(jnp.float32)
+    own_part[...] = shares[col] + share_near[z_hi] + cands[col].astype(jnp.float32)
     for kind in (0, 1, 2):
         share_copy(z_hi, kind).wait_recv()
         own_part[...] += share_in[kind].astype(jnp.float32)
@@ -408,22 +467,29 @@
         share_across(slot).wait_send()
 
 
-def layer(table, w_kv, w_qu, w_out, cand_slice, msg):
+def layer(events, cand_ids, cand_row, wanted, table, w_kv, w_qu, w_out):
     vmem = pl.BlockSpec(memory_space=pltpu.VMEM)
+    anywhere = pl.BlockSpec(memory_space=pl.ANY)
     dma = pltpu.SemaphoreType.DMA
     bf16, f32 = jnp.bfloat16, jnp.float32
     return pl.pallas_call(
         layer_kernel,
         out_shape=jax.ShapeDtypeStruct((CAND, DH), bf16),
-        in_specs=[pl.BlockSpec(memory_space=pl.ANY)] + [vmem] * 5,
+        in_specs=[vmem, pl.BlockSpec(memory_space=pltpu.SMEM), vmem, vmem] + [anywhere] * 5,
         out_specs=vmem,
         scratch_shapes=[
+            pltpu.VMEM((2048, 16, 128), bf16),
+            pltpu.VMEM((D, 2 * DH), bf16),
+            pltpu.VMEM((D, 2 * DH), bf16),
+            pltpu.VMEM((DH, D), bf16),
+            pltpu.VMEM((16, 24, 128), f32),
+            pltpu.VMEM((CAND, 128), f32),
             pltpu.VMEM((8, CHUNK, 128), bf16),
             pltpu.VMEM((8, CAND, 128), bf16),
             pltpu.VMEM((CHUNK, DH), bf16),
             pltpu.VMEM((CHUNK, DH), bf16),
             pltpu.VMEM((16 * CAND, DH), bf16),
-            pltpu.VMEM((16, 16, CAND), f32),
+            pltpu.VMEM((16, 24, 128), f32),
             pltpu.VMEM((DH, CHUNK), bf16),
             pltpu.VMEM((16 * CAND, DH), bf16),
             pltpu.VMEM((CAND, DH), f32),
@@ -456,32 +522,29 @@
             dma((3,)),
             dma((4,)),
             dma((4,)),
-            dma((1,)),
+            dma((4,)),
         ],
         compiler_params=pltpu.CompilerParams(
-            collective_id=0, has_side_effects=True, vmem_limit_bytes=48 << 20
+            collective_id=0, has_side_effects=True, vmem_limit_bytes=60 << 20
         ),
         cost_estimate=pl.CostEstimate(
             flops=8 << 30, bytes_accessed=4 << 20, transcendentals=8 << 20
         ),
         name="layer",
-    )(table, w_kv, w_qu, w_out, cand_slice, msg)
+    )(events, cand_ids, cand_row, wanted, table, table.reshape(2048, 16, 128), w_kv, w_qu, w_out)
 
 
 def on_device(event_ids, cand_ids, cand_request, table, w_kv, w_qu, w_out):
-    cand_slice = jnp.take(table, cand_ids, axis=0)
-    high = (event_ids[None, :] // 128 == jnp.arange(256, dtype=jnp.int32)[:, None]).astype(
-        jnp.bfloat16
+    return layer(
+        event_ids.reshape(1, HIST),
+        cand_ids,
+        cand_ids.reshape(1, CAND),
+        cand_request.reshape(2, 128),
+        table,
+        w_kv,
+        w_qu,
+        w_out,
     )
-    low = (event_ids[None, :] % 128 == jnp.arange(128, dtype=jnp.int32)[:, None]).astype(
-        jnp.bfloat16
-    )
-    times = lax.dot_general(high, low, NT, preferred_element_type=jnp.float32)
-    wanted = (cand_request % REQ_GROUP).astype(jnp.float32)
-    msg = jnp.concatenate(
-        [times.reshape(16, 8, 256), jnp.broadcast_to(wanted[None, None, :], (16, 8, 256))], 1
-    )
-    return layer(table, w_kv, w_qu, w_out, cand_slice, msg)
 
 
 def solution(mesh):

time: 130 us -> 114 us (0.88)
  local copies, waits for them, and re-layouts: 8.9 us -> 1.47 us
  Pallas kernels: 117 us -> 112 us
  other arithmetic: 2.9 us -> 0 us
    gather x1 -> x0, local copies, waits for them, and re-layouts: 5.19 us -> none  [on_device(): cand_slice = jnp.take(table, cand_ids, axis=0)]
    pallas_call x1, Pallas kernels: 117 us -> 112 us  [layer(): pl.pallas_call(layer_kernel, out_shape=jax.ShapeDtypeStruct((CAND, DH), b...]
    unnamed x7 -> x1, local copies, waits for them, and re-layouts: 3.66 us -> 1.47 us
    select_n x3 -> x0, other arithmetic: 1.49 us -> none  [the longest x2 0.79 us: on_device(): cand_slice = jnp.take(table, cand_ids, axis=0)]
where the time goes in v3:
time: 114 us
  Pallas kernels  112 us (98%)
  local copies, waits for them, and re-layouts  1.47 us (1%)
    pallas_call x1, Pallas kernels, layer(): pl.pallas_call(layer_kernel, out_shape=jax.ShapeDtypeStruct((CAND, DH), b...  112 us

profile of v3, /device:TPU:1, one launch (start us, length us, event | category | flops | bytes accessed | tf_op | source)
XLA Modules:
  0.0 113.8 jit_solution(1371181808456191987)
XLA Ops:
  0.0 112.3 %layer.1 = bf16[256,128]{1,0:T(8,128)(2,1)} custom-call(s32[1,2048]{1,0:T(1,128)} %bitcast.5, s32[256]{0:T(256)} %cand_ids.1, s32[1,256]{1,0:T(1,128)} %bitcast.6, s32[2,128]{1,0:T(2,128)} %bitcast.7, bf16[32768,128]{1,0:T(8,128)(2,1)} %table.1, bf16[2048,16,128]{2,1,0:T(8,128)(2,1)} %bitcast.4, bf16[1024,256]{1,0:T(8,128)(2,1)} %w_kv_in.1, ...), custom_call_target="tpu_custom_call" | custom-call | flops 8589934592 | bytes 4194304 | tf_op jit(solution)/shard_map/layer/pallas_call | solution.py:475
  112.4 1.5 %copy.9 = bf16[256,128]{1,0:T(8,128)(2,1)} copy(bf16[256,128]{1,0:T(8,128)(2,1)} %layer.1) | data formatting | bytes 131072

commit v4 on v3

--- a/solution.py
+++ b/solution.py
@@ -65,26 +65,6 @@
             device_id_type=MESH,
         )
 
-    barrier = pltpu.get_barrier_semaphore()
-    for other in (above, below):
-        pl.semaphore_signal(barrier, inc=1, device_id=other, device_id_type=MESH)
-
-    def greet(j, carry):
-        pl.semaphore_signal(
-            barrier, inc=1, device_id=peer(lax.rem(me + j, 16)), device_id_type=MESH
-        )
-        return carry
-
-    lax.fori_loop(1, 16, greet, 0)
-
-    def greet_column(j, carry):
-        pl.semaphore_signal(
-            barrier, inc=1, device_id=(lax.rem(col + j, 8), req), device_id_type=MESH
-        )
-        return carry
-
-    lax.fori_loop(1, 8, greet_column, 0)
-
     def place(block, half, p):
         return rows.at[block * 2 + half, pl.ds(pl.multiple_of(p * ROWS, ROWS), ROWS), :]
 
@@ -103,70 +83,25 @@
     for copy in (table_copy, qu_copy, kv_copy, out_copy):
         copy.start()
 
-    place_in = (cand_row[...] & 15).astype(jnp.float32)
-    within[...] = jnp.broadcast_to(place_in, (128, CAND)).T
-    lane = lax.broadcasted_iota(jnp.int32, (16, 256), 1)
-    lane = (lane - 16 * lax.broadcasted_iota(jnp.int32, (16, 256), 0)).astype(jnp.float32)
-    table_copy.wait()
-
-    def look_up(g, carry):
-        for k in range(4):
-            first = pl.multiple_of(g * 64 + k * 16, 16)
-            tiles = [table_here[cand_ids[first + i] >> 4] for i in range(16)]
-            wide = within[pl.ds(first, 16), :]
-            pick = jnp.where(lane == jnp.concatenate([wide, wide], 1), 1.0, 0.0).astype(jnp.bfloat16)
-            found = jnp.dot(pick, jnp.concatenate(tiles, 0), preferred_element_type=jnp.float32)
-            cands[col, pl.ds(first, 16), :] = found.astype(jnp.bfloat16)
-        return carry
-
-    lax.fori_loop(0, 4, look_up, 0)
-    pl.semaphore_wait(barrier, 24)
-
-    def cand_copy(block, target, kind):
-        slot = cands.at[block * 2 + core]
-        return remote(slot, slot, c_send.at[kind], c_recv.at[kind], column(target))
-
-    cand_copy(z_hi, above_block, 0).start()
-    cand_copy(z_hi, below_block, 1).start()
-    cand_copy(z_hi, far_block, 2).start()
-
-    def cand_across(block, slot):
-        ref = cands.at[block * 2 + core]
-        return remote(ref, ref, cp_send.at[slot], cp_recv.at[slot], sibling)
-
-    cand_across(z_hi, 0).start()
-
-    def ring(block, p, target, kind):
-        ref = place(block, core, p)
-        return remote(ref, ref, ring_send.at[kind, p], ring_recv.at[kind, p], target)
-
-    def across(block, p, slot):
-        ref = place(block, core, p)
-        return remote(ref, ref, pair_send.at[slot, p], pair_recv.at[slot, p], sibling)
-
-    half = PIECES // 2
-
-    def in_turn(i, first):
-        return jnp.where(i < half, 2 * i + first, 2 * (i - half) + 1 - first)
-
-    def own_here(p, carry):
-        own_copy(p).wait()
-        across(z_hi, p, 0).start()
-        return carry
-
-    def send_own(i, carry):
-        @pl.when(z_lo == 3)
-        def _():
-            ring(z_hi, in_turn(i, 0), above, 0).start()
-
-        @pl.when(z_lo == 0)
-        def _():
-            ring(z_hi, in_turn(i, 1), below, 1).start()
-
-        return carry
-
-    lax.fori_loop(0, PIECES, own_here, 0)
-    lax.fori_loop(0, PIECES, send_own, 0)
+    barrier = pltpu.get_barrier_semaphore()
+    def greet_column(j, carry):
+        pl.semaphore_signal(
+            barrier, inc=1, device_id=(lax.rem(col + j, 8), req), device_id_type=MESH
+        )
+        return carry
+
+    lax.fori_loop(1, 8, greet_column, 0)
+
+    for other in (above, below):
+        pl.semaphore_signal(barrier, inc=1, device_id=other, device_id_type=MESH)
+
+    def greet(j, carry):
+        pl.semaphore_signal(
+            barrier, inc=1, device_id=peer(lax.rem(me + j, 16)), device_id_type=MESH
+        )
+        return carry
+
+    lax.fori_loop(1, 16, greet, 0)
 
     times = jnp.zeros((256, 128), jnp.float32)
     for k in range(4):
@@ -186,6 +121,71 @@
         msg_out[k, 18:24, :] = jnp.zeros((6, 128), jnp.float32)
     msgs[me] = msg_out[me]
 
+    place_in = (cand_row[...] & 15).astype(jnp.float32)
+    within[...] = jnp.broadcast_to(place_in, (128, CAND)).T
+    lane = lax.broadcasted_iota(jnp.int32, (16, 256), 1)
+    lane = (lane - 16 * lax.broadcasted_iota(jnp.int32, (16, 256), 0)).astype(jnp.float32)
+    table_copy.wait()
+
+    def look_up(g, carry):
+        for k in range(4):
+            first = pl.multiple_of(g * 64 + k * 16, 16)
+            tiles = [table_here[cand_ids[first + i] >> 4] for i in range(16)]
+            wide = within[pl.ds(first, 16), :]
+            pick = jnp.where(lane == jnp.concatenate([wide, wide], 1), 1.0, 0.0).astype(jnp.bfloat16)
+            found = jnp.dot(pick, jnp.concatenate(tiles, 0), preferred_element_type=jnp.float32)
+            cands[col, pl.ds(first, 16), :] = found.astype(jnp.bfloat16)
+        return carry
+
+    lax.fori_loop(0, 4, look_up, 0)
+    pl.semaphore_wait(barrier, 24)
+
+    def cand_copy(block, target, kind):
+        slot = cands.at[block * 2 + core]
+        return remote(slot, slot, c_send.at[kind], c_recv.at[kind], column(target))
+
+    cand_copy(z_hi, above_block, 0).start()
+    cand_copy(z_hi, below_block, 1).start()
+    cand_copy(z_hi, far_block, 2).start()
+
+    def cand_across(block, slot):
+        ref = cands.at[block * 2 + core]
+        return remote(ref, ref, cp_send.at[slot], cp_recv.at[slot], sibling)
+
+    cand_across(z_hi, 0).start()
+
+    def ring(block, p, target, kind):
+        ref = place(block, core, p)
+        return remote(ref, ref, ring_send.at[kind, p], ring_recv.at[kind, p], target)
+
+    def across(block, p, slot):
+        ref = place(block, core, p)
+        return remote(ref, ref, pair_send.at[slot, p], pair_recv.at[slot, p], sibling)
+
+    half = PIECES // 2
+
+    def in_turn(i, first):
+        return jnp.where(i < half, 2 * i + first, 2 * (i - half) + 1 - first)
+
+    def own_here(p, carry):
+        own_copy(p).wait()
+        across(z_hi, p, 0).start()
+        return carry
+
+    def send_own(i, carry):
+        @pl.when(z_lo == 3)
+        def _():
+            ring(z_hi, in_turn(i, 0), above, 0).start()
+
+        @pl.when(z_lo == 0)
+        def _():
+            ring(z_hi, in_turn(i, 1), below, 1).start()
+
+        return carry
+
+    lax.fori_loop(0, PIECES, own_here, 0)
+    lax.fori_loop(0, PIECES, send_own, 0)
+
     def m_copy(j, slot):
         to = lax.rem(me + j, 16)
         return remote(msg_out.at[to], msgs.at[slot], m_send.at[j], m_recv.at[slot], peer(to))
@@ -204,6 +204,10 @@
         return carry
 
     lax.fori_loop(1, 16, spread_m, 0)
+
+    def messages(j, carry):
+        m_copy(j, lax.rem(me + j, 16)).wait_recv()
+        return carry
 
     up_lag, down_lag = LAG * z_lo, LAG * (3 - z_lo)
 
@@ -290,6 +294,17 @@
             queries[mine, :] = both[:, :DH].astype(jnp.bfloat16)
             gate[...] = both[:, DH:]
             lax.fori_loop(1, 16, spread_q, 0)
+
+        @pl.when(t == 7 * LAG)
+        def _():
+            lax.fori_loop(1, 16, messages, 0)
+            for s in range(16):
+                count = msgs[:, s, :]
+                high = jnp.floor(count * (1.0 / 256.0))
+                low = count - high * 256.0
+                counts[:, s * 128 : (s + 1) * 128] = jnp.concatenate(
+                    [low, high, jnp.zeros((96, 128), jnp.float32)], 0
+                ).astype(jnp.bfloat16)
 
         i4 = t - 7 * LAG - 1
 
@@ -311,30 +326,20 @@
     lax.fori_loop(0, PIECES // 2 + 7 * LAG + 1, ring_step, 0)
 
     def arrived(j, carry):
-        src = lax.rem(me + j, 16)
-        m_copy(j, src).wait_recv()
-        q_copy(j, src).wait_recv()
+        q_copy(j, lax.rem(me + j, 16)).wait_recv()
         return carry
 
     lax.fori_loop(1, 16, arrived, 0)
-    for s in range(16):
-        count = msgs[:, s, :]
-        high = jnp.floor(count * (1.0 / 256.0))
-        low = count - high * 256.0
-        counts[:, s * 128 : (s + 1) * 128] = jnp.concatenate(
-            [low, high, jnp.zeros((96, 128), jnp.float32)], 0
-        ).astype(jnp.bfloat16)
-
-    def mark(src, carry):
+
+    def mark(pair):
         lane = lax.broadcasted_iota(jnp.int32, (DH, 128), 0).astype(jnp.float32)
-        for k in range(2):
-            wanted = msgs[src, 16 + k : 17 + k, :]
+        for k in range(4):
+            wanted = msgs[pair * 2 + k // 2, 16 + k % 2 : 17 + k % 2, :]
             hot = jnp.where(lane == wanted, 1.0, 0.0) + jnp.where(lane == wanted + 16.0, 256.0, 0.0)
-            start = pl.multiple_of(src * CAND + k * 128, 128)
+            start = pl.multiple_of(pair * PAIR + k * 128, 128)
             onehot[pl.ds(start, 128), :] = hot.T.astype(jnp.bfloat16)
-        return carry
-
-    lax.fori_loop(0, 16, mark, 0)
+
+    mark(lax.rem(me // 2 + 1, 8))
 
     half_scale = 0.5 / math.sqrt(DH)
 
@@ -345,6 +350,7 @@
         pair = lax.rem(me // 2 + 1 + i, 8)
         here = pl.ds(pl.multiple_of(pair * PAIR, PAIR), PAIR)
         picked, hot = queries[here, :], onehot[here, :]
+        mark(lax.rem(me // 2 + 2 + i, 8))
         total = jnp.zeros((PAIR, DH), jnp.float32)
         for r in range(CHUNK // TILE):
             span = slice(r * TILE, (r + 1) * TILE)
@@ -370,13 +376,17 @@
 
     lax.fori_loop(0, 8, attend_pair, 0)
 
-    def collect(j, carry):
-        src = lax.rem(me + j, 16)
-        part_copy(src, src).wait_recv()
-        own_part[...] += parts_in[src].astype(jnp.float32)
-        return carry
-
-    lax.fori_loop(1, 16, collect, 0)
+    def collect(d, carry):
+        src = lax.rem(me // 2 + 8 - d, 8) * 2
+        for k in range(2):
+            part_copy(src + k, src + k).wait_recv()
+        own_part[...] += parts_in[src].astype(jnp.float32) + parts_in[src + 1].astype(jnp.float32)
+        return carry
+
+    lax.fori_loop(1, 8, collect, 0)
+    beside = me + 1 - 2 * lax.rem(me, 2)
+    part_copy(beside, beside).wait_recv()
+    own_part[...] += parts_in[beside].astype(jnp.float32)
 
     attended = (own_part[...] * (1.0 / HIST)).T
     moments[col, 0:1, :] = jnp.sum(attended, axis=0, keepdims=True)

time: 114 us -> 112 us (0.982)
  Pallas kernels: 112 us -> 110 us
    pallas_call x1, Pallas kernels: 112 us -> 110 us  [layer(): pl.pallas_call(layer_kernel, out_shape=jax.ShapeDtypeStruct((CAND, DH), b...]
where the time goes in v4:
time: 112 us
  Pallas kernels  110 us (98%)
  local copies, waits for them, and re-layouts  1.47 us (1%)
    pallas_call x1, Pallas kernels, layer(): pl.pallas_call(layer_kernel, out_shape=jax.ShapeDtypeStruct((CAND, DH), b...  110 us

profile of v4, /device:TPU:1, one launch (start us, length us, event | category | flops | bytes accessed | tf_op | source)
XLA Modules:
  0.0 111.7 jit_solution(12754499178686503034)
XLA Ops:
  0.0 110.3 %layer.1 = bf16[256,128]{1,0:T(8,128)(2,1)} custom-call(s32[1,2048]{1,0:T(1,128)} %bitcast.5, s32[256]{0:T(256)} %cand_ids.1, s32[1,256]{1,0:T(1,128)} %bitcast.6, s32[2,128]{1,0:T(2,128)} %bitcast.7, bf16[32768,128]{1,0:T(8,128)(2,1)} %table.1, bf16[2048,16,128]{2,1,0:T(8,128)(2,1)} %bitcast.4, bf16[1024,256]{1,0:T(8,128)(2,1)} %w_kv_in.1, ...), custom_call_target="tpu_custom_call" | custom-call | flops 8589934592 | bytes 4194304 | tf_op jit(solution)/shard_map/layer/pallas_call | solution.py:485
  110.3 1.5 %copy.9 = bf16[256,128]{1,0:T(8,128)(2,1)} copy(bf16[256,128]{1,0:T(8,128)(2,1)} %layer.1) | data formatting | bytes 131072

commit v5 on v4

--- a/solution.py
+++ b/solution.py
@@ -15,11 +15,11 @@
 REQ_GROUP = 16
 CHUNK = 2048
 CAND = 256
-PIECES = 8
+PIECES = 16
 ROWS = CHUNK // PIECES
-LAG = 2
-CAND_STEP = 3
-FAR_STEP = 5
+LAG = 4
+CAND_STEP = 6
+FAR_STEP = 9
 PAIR = 2 * CAND
 TILE = 512
 MESH = pl.DeviceIdType.MESH
@@ -418,9 +418,10 @@
     gated = ((attended - average) * lax.rsqrt(variance + 1e-05) * gate_t).T.astype(jnp.bfloat16)
 
     out_copy.wait()
-    product = jnp.dot(gated, w_out[...], preferred_element_type=jnp.float32)
-    for k in range(8):
-        shares[k] = product[:, k * 128 : (k + 1) * 128]
+
+    def project(slot):
+        columns = w_out[:, pl.ds(pl.multiple_of(slot * 128, 128), 128)]
+        shares[slot] = jnp.dot(gated, columns, preferred_element_type=jnp.float32)
 
     def share_across(block):
         return remote(
@@ -435,7 +436,10 @@
 
     order = ((far_block, 2), (above_block, 0), (below_block, 1))
     for block, _ in order + ((z_hi, 3),):
+        project(block * 2 + 1 - core)
         share_across(block).start()
+    for block, _ in order + ((z_hi, 3),):
+        project(block * 2 + core)
     for block, kind in order:
         share_across(block).wait_recv()
         share_out[kind] = (shares[block * 2 + core] + share_near[block]).astype(jnp.bfloat16)

time: 112 us -> 112 us (level)
  no operation moved by 1% of the time
where the time goes in v5:
time: 112 us; the launch traced here: 111 us
  Pallas kernels  110 us (98%)
  local copies, waits for them, and re-layouts  1.47 us (1%)
    pallas_call x1, Pallas kernels, layer(): pl.pallas_call(layer_kernel, out_shape=jax.ShapeDtypeStruct((CAND, DH), b...  110 us

profile of v5, /device:TPU:1, one launch (start us, length us, event | category | flops | bytes accessed | tf_op | source)
XLA Modules:
  0.0 111.0 jit_solution(1865127511865974082)
XLA Ops:
  0.0 109.5 %layer.1 = bf16[256,128]{1,0:T(8,128)(2,1)} custom-call(s32[1,2048]{1,0:T(1,128)} %bitcast.5, s32[256]{0:T(256)} %cand_ids.1, s32[1,256]{1,0:T(1,128)} %bitcast.6, s32[2,128]{1,0:T(2,128)} %bitcast.7, bf16[32768,128]{1,0:T(8,128)(2,1)} %table.1, bf16[2048,16,128]{2,1,0:T(8,128)(2,1)} %bitcast.4, bf16[1024,256]{1,0:T(8,128)(2,1)} %w_kv_in.1, ...), custom_call_target="tpu_custom_call" | custom-call | flops 8589934592 | bytes 4194304 | tf_op jit(solution)/shard_map/layer/pallas_call | solution.py:489
  109.5 1.5 %copy.9 = bf16[256,128]{1,0:T(8,128)(2,1)} copy(bf16[256,128]{1,0:T(8,128)(2,1)} %layer.1) | data formatting | bytes 131072
